TPU v7x, 256 devices: a whole 4x4x8 slice. The times are simulated.
256 devices in a mesh: vec: 32 (over y, z), field: 4 (over x_lo, core), rep: 2 (over x_hi).
Axes of the slice: x: 4 (x_hi: 2, x_lo: 2; x = x_hi * 2 + x_lo), y: 4, z: 8, core: 2. Of those that a mesh axis runs over, the one named last changes fastest.
Arguments:
- dosage: bfloat16 [768, 65536], P('vec', 'field'), may hold values from 0 to 2
Outputs:
- ccc: float32 [2, 768, 2, 24, 2, 96], P('rep', ('vec', 'field'))
All inputs are finite; a program needn't handle non-finite values.
Results may differ from a plain program's by a relative error of at most 0.0003.
Values may be sent and summed in bfloat16 or wider, within the bound.
No kernel may reach another device: no remote copies, remote signals or barrier semaphores. Data moves between devices by JAX's collectives and lax.ppermute only.
A program may use at most 64 MiB of HBM per device.

v0:
```python
import jax
import jax.numpy as jnp
from jax import lax
from jax.sharding import PartitionSpec as P

F = 65536
S = 2


def passed_along(value, axis, by):
    count = lax.axis_size(axis)
    return lax.ppermute(value, axis, [(i, (i + by) % count) for i in range(count)])


def sent_to_all(value, axis):
    copies = jnp.broadcast_to(value, (lax.axis_size(axis), *value.shape))
    return lax.all_to_all(copies, axis, split_axis=0, concat_axis=0, tiled=True)


def of_everyone(value, axis):
    return sent_to_all(value, axis).sum(axis=0)


def packed_total(arrays, axis):
    flat, at, finished = (jnp.concatenate([a.reshape(-1) for a in arrays]), 0, [])
    running = of_everyone(flat, axis)
    for a in arrays:
        finished.append(running[at : at + a.size].reshape(a.shape))
        at += a.size
    return tuple(finished)


def in_blocks(value, dim, count):
    before, after = (value.shape[:dim], value.shape[dim + 1 :])
    return jnp.moveaxis(value.reshape(*before, count, -1, *after), dim, 0)


def sum_at_owner(value, axis, dim):
    blocks = in_blocks(value, dim, lax.axis_size(axis))
    arrived = lax.all_to_all(blocks, axis, split_axis=0, concat_axis=0, tiled=True)
    return arrived.sum(axis=0)


def contract(first_rows, third_rows, partner_rows):
    field_width = first_rows.shape[1]
    block_width = min(1024, field_width)
    block_count = field_width // block_width

    def add_block(block_id, running):
        offset = block_id * block_width
        first_cut = lax.dynamic_slice_in_dim(first_rows, offset, block_width, 1)
        third_cut = lax.dynamic_slice_in_dim(third_rows, offset, block_width, 1)
        partner_cut = lax.dynamic_slice_in_dim(partner_rows, offset, block_width, 1)
        pair_rows = (first_cut[:, None, :] * third_cut[None, :, :]).reshape(-1, block_width)
        return running + lax.dot_general(
            pair_rows, partner_cut, (((1,), (1,)), ((), ())), preferred_element_type=jnp.float32
        )

    start_value = jnp.zeros(
        (first_rows.shape[0] * third_rows.shape[0], partner_rows.shape[0]), jnp.float32
    )
    return lax.fori_loop(0, block_count, add_block, start_value)


def row_totals(rows):
    return jnp.sum(rows.astype(jnp.float32), axis=1)


def body(dosage):
    vectors = dosage.shape[0]
    field_place = lax.axis_index("field")
    share_rows = vectors // lax.axis_size("field")
    rep_plane = lax.axis_index("rep")
    other_count = (2.0 - dosage.astype(jnp.float32)).astype(jnp.bfloat16)
    stacked = jnp.stack([other_count, dosage], axis=1)
    vector_rows = stacked.reshape(2 * vectors, dosage.shape[1])
    third_near = passed_along(vector_rows, "vec", 1)
    third_far = passed_along(third_near, "vec", 1)
    third_rows = jnp.where(rep_plane == 0, third_near, third_far)
    partners = []
    current = vector_rows
    for hop_count in range(S):
        current = passed_along(current, "vec", -1)
        partners.append(current)
    partner_rows = jnp.concatenate(partners, axis=0)
    own_total, third_total, partner_total = packed_total(
        (row_totals(vector_rows), row_totals(third_rows), row_totals(partner_rows)), "field"
    )
    gain_own = (1.0 - own_total / (3.0 * F)).reshape(vectors, 2)
    gain_third = (1.0 - third_total / (3.0 * F)).reshape(vectors, 2)
    gain_partner = 1.0 - partner_total / (3.0 * F)
    tables = contract(vector_rows, third_rows, partner_rows)
    tables = tables.reshape(vectors, 2, vectors, 2, tables.shape[1])
    summed = sum_at_owner(tables, "field", 0)
    gain_first = lax.dynamic_slice_in_dim(gain_own, field_place * share_rows, share_rows, 0)
    result = (
        4.5
        / (8.0 * F)
        * summed
        * gain_first[:, :, None, None, None]
        * gain_third[None, None, :, :, None]
        * gain_partner
    )
    return result[None]


def solution(mesh):
    placed = (P("vec", "field"),)
    return jax.shard_map(
        body,
        mesh=mesh,
        in_specs=placed,
        out_specs=P("rep", ("vec", "field"), None, None, None, None),
        check_vma=False,
    )
```

profile of v0, /device:TPU:1, one launch (start us, length us, event | category | flops | bytes accessed | tf_op | source)
XLA Modules:
  0.0 185.8 jit_solution(17152526004299796799)
XLA Ops:
  0.0 1.3 fusion.2
  1.5 2.8 %copy.11 = bf16[24,2,16384]{2,1,0:T(2,128)(2,1)} copy(bf16[24,2,16384]{2,0,1:T(8,128)(2,1)S(1)} %pad_maximum_fusion) | data formatting | bytes 3145728 | tf_op jit(solution)/shard_map/stack | solution.py:75
  4.3 3.6 %reshape.65 = bf16[48,16384]{1,0:T(8,128)(2,1)} reshape(bf16[24,2,16384]{2,1,0:T(2,128)(2,1)} %copy.11) | data formatting | bytes 3145728 | tf_op jit(solution)/shard_map/reshape | solution.py:76
  7.9 8.9 %collective-permute-start.2 = (bf16[48,16384]{1,0:T(8,128)(2,1)}, bf16[48,16384]{1,0:T(8,128)(2,1)}, u32[]{:S(2)}, u32[]{:S(2)}) collective-permute-start(bf16[48,16384]{1,0:T(8,128)(2,1)} %reshape.65), channel_id=1, source_target_pairs={{0,248},{8,0},{16,8},{24,16},{32,24},{40,32},{48,40},{56,48},{64,5... | collective-permute-start | bytes 4718600 | tf_op jit(solution)/shard_map/ppermute | solution.py:12
  17.3 32.8 %collective-permute-done.2 = bf16[48,16384]{1,0:T(8,128)(2,1)} collective-permute-done((bf16[48,16384]{1,0:T(8,128)(2,1)}, bf16[48,16384]{1,0:T(8,128)(2,1)}, u32[]{:S(2)}, u32[]{:S(2)}) %collective-permute-start.2) | collective-permute-done | bytes 1572896 | tf_op jit(solution)/shard_map/ppermute | solution.py:12
  50.2 5.5 %collective-permute-start.3 = (bf16[48,16384]{1,0:T(8,128)(2,1)}, bf16[48,16384]{1,0:T(8,128)(2,1)S(1)}, u32[]{:S(2)}, u32[]{:S(2)}) collective-permute-start(bf16[48,16384]{1,0:T(8,128)(2,1)} %collective-permute-done.2), channel_id=1, source_target_pairs={{0,248},{8,0},{16,8},{24,16},{32,24},{40,32},{48,40},{56,48},{64,5... | collective-permute-start | bytes 4718600 | tf_op jit(solution)/shard_map/ppermute | solution.py:12
  55.7 1.5 constant_dynamic-update-slice_fusion.1
  57.2 30.9 %collective-permute-done.3 = bf16[48,16384]{1,0:T(8,128)(2,1)S(1)} collective-permute-done((bf16[48,16384]{1,0:T(8,128)(2,1)}, bf16[48,16384]{1,0:T(8,128)(2,1)S(1)}, u32[]{:S(2)}, u32[]{:S(2)}) %collective-permute-start.3) | collective-permute-done | bytes 1572896 | tf_op jit(solution)/shard_map/ppermute | solution.py:12
  88.7 1.2 copy-done
  89.9 3.4 %collective-permute-done.1 = bf16[48,16384]{1,0:T(8,128)(2,1)S(1)} collective-permute-done((bf16[48,16384]{1,0:T(8,128)(2,1)}, bf16[48,16384]{1,0:T(8,128)(2,1)S(1)}, u32[]{:S(2)}, u32[]{:S(2)}) %collective-permute-start.1) | collective-permute-done | bytes 1572896 | tf_op jit(solution)/shard_map/ppermute | solution.py:12
  93.3 2.1 %convert_reduce_fusion.1 = (f32[48]{0:T(128)S(1)}, bf16[48,16384]{1,0:T(8,128)(2,1)S(1)}) fusion(bf16[48,16384]{1,0:T(8,128)(2,1)} %collective-permute-done, bf16[48,16384]{1,0:T(8,128)(2,1)S(1)} %collective-permute-done.1, pred[]{:T(512)S(6)} %eq.3), kind=kLoop, calls=%fused_computation.7 | loop fusion | flops 2359248 | bytes 4718785 | tf_op jit(solution)/shard_map/reduce_sum | solution.py:66
  96.0 6.0 %all-to-all-start.1 = ((f32[4,1,192]{2,1,0:T(1,128)}), f32[4,1,192]{2,1,0:T(1,128)S(1)}, u32[]{:S(2)}, u32[]{:S(2)}) async-start(f32[4,1,192]{2,1,0:T(1,128)} %broadcast_in_dim.16), calls=%async_computation.1 | async-start | bytes 8192 | tf_op jit(solution)/shard_map/all_to_all | solution.py:17
  102.0 62.1 %while.14 = (s32[]{:T(128)}, f32[2304,96]{0,1:T(8,128)S(1)}, bf16[48,16384]{1,0:T(8,128)(2,1)}, bf16[48,16384]{1,0:T(8,128)(2,1)S(1)}, bf16[96,16384]{1,0:T(8,12...) while((s32[]{:T(128)}, f32[2304,96]{0,1:T(8,128)S(1)}, bf16[48,16384]{1,0:T(8,128)(2,1)}, ...), condition=%wide.region_1.2_spmd.clone, body=%wide.region_0.1_spmd.clone.sunk | while | flops 455786496 | bytes 11993253 | solution.py:62
  103.2 2.6 %convolution_add_fusion.2 = f32[2304,96]{0,1:T(8,128)S(1)} fusion(bf16[2304,1024]{1,0:T(8,128)(2,1)S(1)} %bitcast.16, f32[2304,96]{0,1:T(8,128)S(1)} %get-tuple-element.179, pred[]{:T(512)S(6)} %compare.3, bf16[96,16384]{1,0:T(8,128)(2,1)} %get-tuple-element.191, s32[]{:T(128)S(6)} %select_n.29), kind=kOutput, calls=%fused_computation.clone.1 | convolution fusion | flops 453427200 | bytes 6684677 | tf_op jit(solution)/shard_map/while/body/eval_jaxpr/dot_general | solution.py:55
  105.9 0.9 constant_dynamic-slice_fusion.3
  107.1 2.6 %convolution_add_fusion.2 = f32[2304,96]{0,1:T(8,128)S(1)} fusion(bf16[2304,1024]{1,0:T(8,128)(2,1)S(1)} %bitcast.16, f32[2304,96]{0,1:T(8,128)S(1)} %get-tuple-element.179, pred[]{:T(512)S(6)} %compare.3, bf16[96,16384]{1,0:T(8,128)(2,1)} %get-tuple-element.191, s32[]{:T(128)S(6)} %select_n.29), kind=kOutput, calls=%fused_computation.clone.1 | convolution fusion | flops 453427200 | bytes 6684677 | tf_op jit(solution)/shard_map/while/body/eval_jaxpr/dot_general | solution.py:55
  109.8 0.9 constant_dynamic-slice_fusion.3
  111.0 2.6 %convolution_add_fusion.2 = f32[2304,96]{0,1:T(8,128)S(1)} fusion(bf16[2304,1024]{1,0:T(8,128)(2,1)S(1)} %bitcast.16, f32[2304,96]{0,1:T(8,128)S(1)} %get-tuple-element.179, pred[]{:T(512)S(6)} %compare.3, bf16[96,16384]{1,0:T(8,128)(2,1)} %get-tuple-element.191, s32[]{:T(128)S(6)} %select_n.29), kind=kOutput, calls=%fused_computation.clone.1 | convolution fusion | flops 453427200 | bytes 6684677 | tf_op jit(solution)/shard_map/while/body/eval_jaxpr/dot_general | solution.py:55
  113.6 0.9 constant_dynamic-slice_fusion.3
  114.9 2.6 %convolution_add_fusion.2 = f32[2304,96]{0,1:T(8,128)S(1)} fusion(bf16[2304,1024]{1,0:T(8,128)(2,1)S(1)} %bitcast.16, f32[2304,96]{0,1:T(8,128)S(1)} %get-tuple-element.179, pred[]{:T(512)S(6)} %compare.3, bf16[96,16384]{1,0:T(8,128)(2,1)} %get-tuple-element.191, s32[]{:T(128)S(6)} %select_n.29), kind=kOutput, calls=%fused_computation.clone.1 | convolution fusion | flops 453427200 | bytes 6684677 | tf_op jit(solution)/shard_map/while/body/eval_jaxpr/dot_general | solution.py:55
  117.5 0.9 constant_dynamic-slice_fusion.3
  118.8 2.6 %convolution_add_fusion.2 = f32[2304,96]{0,1:T(8,128)S(1)} fusion(bf16[2304,1024]{1,0:T(8,128)(2,1)S(1)} %bitcast.16, f32[2304,96]{0,1:T(8,128)S(1)} %get-tuple-element.179, pred[]{:T(512)S(6)} %compare.3, bf16[96,16384]{1,0:T(8,128)(2,1)} %get-tuple-element.191, s32[]{:T(128)S(6)} %select_n.29), kind=kOutput, calls=%fused_computation.clone.1 | convolution fusion | flops 453427200 | bytes 6684677 | tf_op jit(solution)/shard_map/while/body/eval_jaxpr/dot_general | solution.py:55
  121.4 0.9 constant_dynamic-slice_fusion.3
  122.6 2.6 %convolution_add_fusion.2 = f32[2304,96]{0,1:T(8,128)S(1)} fusion(bf16[2304,1024]{1,0:T(8,128)(2,1)S(1)} %bitcast.16, f32[2304,96]{0,1:T(8,128)S(1)} %get-tuple-element.179, pred[]{:T(512)S(6)} %compare.3, bf16[96,16384]{1,0:T(8,128)(2,1)} %get-tuple-element.191, s32[]{:T(128)S(6)} %select_n.29), kind=kOutput, calls=%fused_computation.clone.1 | convolution fusion | flops 453427200 | bytes 6684677 | tf_op jit(solution)/shard_map/while/body/eval_jaxpr/dot_general | solution.py:55
  125.3 0.9 constant_dynamic-slice_fusion.3
  126.5 2.6 %convolution_add_fusion.2 = f32[2304,96]{0,1:T(8,128)S(1)} fusion(bf16[2304,1024]{1,0:T(8,128)(2,1)S(1)} %bitcast.16, f32[2304,96]{0,1:T(8,128)S(1)} %get-tuple-element.179, pred[]{:T(512)S(6)} %compare.3, bf16[96,16384]{1,0:T(8,128)(2,1)} %get-tuple-element.191, s32[]{:T(128)S(6)} %select_n.29), kind=kOutput, calls=%fused_computation.clone.1 | convolution fusion | flops 453427200 | bytes 6684677 | tf_op jit(solution)/shard_map/while/body/eval_jaxpr/dot_general | solution.py:55
  129.2 0.9 constant_dynamic-slice_fusion.3
  130.4 2.6 %convolution_add_fusion.2 = f32[2304,96]{0,1:T(8,128)S(1)} fusion(bf16[2304,1024]{1,0:T(8,128)(2,1)S(1)} %bitcast.16, f32[2304,96]{0,1:T(8,128)S(1)} %get-tuple-element.179, pred[]{:T(512)S(6)} %compare.3, bf16[96,16384]{1,0:T(8,128)(2,1)} %get-tuple-element.191, s32[]{:T(128)S(6)} %select_n.29), kind=kOutput, calls=%fused_computation.clone.1 | convolution fusion | flops 453427200 | bytes 6684677 | tf_op jit(solution)/shard_map/while/body/eval_jaxpr/dot_general | solution.py:55
  133.0 0.9 constant_dynamic-slice_fusion.3
  134.3 2.6 %convolution_add_fusion.2 = f32[2304,96]{0,1:T(8,128)S(1)} fusion(bf16[2304,1024]{1,0:T(8,128)(2,1)S(1)} %bitcast.16, f32[2304,96]{0,1:T(8,128)S(1)} %get-tuple-element.179, pred[]{:T(512)S(6)} %compare.3, bf16[96,16384]{1,0:T(8,128)(2,1)} %get-tuple-element.191, s32[]{:T(128)S(6)} %select_n.29), kind=kOutput, calls=%fused_computation.clone.1 | convolution fusion | flops 453427200 | bytes 6684677 | tf_op jit(solution)/shard_map/while/body/eval_jaxpr/dot_general | solution.py:55
  136.9 0.9 constant_dynamic-slice_fusion.3
  138.2 2.6 %convolution_add_fusion.2 = f32[2304,96]{0,1:T(8,128)S(1)} fusion(bf16[2304,1024]{1,0:T(8,128)(2,1)S(1)} %bitcast.16, f32[2304,96]{0,1:T(8,128)S(1)} %get-tuple-element.179, pred[]{:T(512)S(6)} %compare.3, bf16[96,16384]{1,0:T(8,128)(2,1)} %get-tuple-element.191, s32[]{:T(128)S(6)} %select_n.29), kind=kOutput, calls=%fused_computation.clone.1 | convolution fusion | flops 453427200 | bytes 6684677 | tf_op jit(solution)/shard_map/while/body/eval_jaxpr/dot_general | solution.py:55
  140.8 0.9 constant_dynamic-slice_fusion.3
  142.0 2.6 %convolution_add_fusion.2 = f32[2304,96]{0,1:T(8,128)S(1)} fusion(bf16[2304,1024]{1,0:T(8,128)(2,1)S(1)} %bitcast.16, f32[2304,96]{0,1:T(8,128)S(1)} %get-tuple-element.179, pred[]{:T(512)S(6)} %compare.3, bf16[96,16384]{1,0:T(8,128)(2,1)} %get-tuple-element.191, s32[]{:T(128)S(6)} %select_n.29), kind=kOutput, calls=%fused_computation.clone.1 | convolution fusion | flops 453427200 | bytes 6684677 | tf_op jit(solution)/shard_map/while/body/eval_jaxpr/dot_general | solution.py:55
  144.7 0.9 constant_dynamic-slice_fusion.3
  145.9 2.6 %convolution_add_fusion.2 = f32[2304,96]{0,1:T(8,128)S(1)} fusion(bf16[2304,1024]{1,0:T(8,128)(2,1)S(1)} %bitcast.16, f32[2304,96]{0,1:T(8,128)S(1)} %get-tuple-element.179, pred[]{:T(512)S(6)} %compare.3, bf16[96,16384]{1,0:T(8,128)(2,1)} %get-tuple-element.191, s32[]{:T(128)S(6)} %select_n.29), kind=kOutput, calls=%fused_computation.clone.1 | convolution fusion | flops 453427200 | bytes 6684677 | tf_op jit(solution)/shard_map/while/body/eval_jaxpr/dot_general | solution.py:55
  148.6 0.9 constant_dynamic-slice_fusion.3
  149.8 2.6 %convolution_add_fusion.2 = f32[2304,96]{0,1:T(8,128)S(1)} fusion(bf16[2304,1024]{1,0:T(8,128)(2,1)S(1)} %bitcast.16, f32[2304,96]{0,1:T(8,128)S(1)} %get-tuple-element.179, pred[]{:T(512)S(6)} %compare.3, bf16[96,16384]{1,0:T(8,128)(2,1)} %get-tuple-element.191, s32[]{:T(128)S(6)} %select_n.29), kind=kOutput, calls=%fused_computation.clone.1 | convolution fusion | flops 453427200 | bytes 6684677 | tf_op jit(solution)/shard_map/while/body/eval_jaxpr/dot_general | solution.py:55
  152.5 0.9 constant_dynamic-slice_fusion.3
  153.7 2.6 %convolution_add_fusion.2 = f32[2304,96]{0,1:T(8,128)S(1)} fusion(bf16[2304,1024]{1,0:T(8,128)(2,1)S(1)} %bitcast.16, f32[2304,96]{0,1:T(8,128)S(1)} %get-tuple-element.179, pred[]{:T(512)S(6)} %compare.3, bf16[96,16384]{1,0:T(8,128)(2,1)} %get-tuple-element.191, s32[]{:T(128)S(6)} %select_n.29), kind=kOutput, calls=%fused_computation.clone.1 | convolution fusion | flops 453427200 | bytes 6684677 | tf_op jit(solution)/shard_map/while/body/eval_jaxpr/dot_general | solution.py:55
  156.3 0.9 constant_dynamic-slice_fusion.3
  157.6 2.6 %convolution_add_fusion.2 = f32[2304,96]{0,1:T(8,128)S(1)} fusion(bf16[2304,1024]{1,0:T(8,128)(2,1)S(1)} %bitcast.16, f32[2304,96]{0,1:T(8,128)S(1)} %get-tuple-element.179, pred[]{:T(512)S(6)} %compare.3, bf16[96,16384]{1,0:T(8,128)(2,1)} %get-tuple-element.191, s32[]{:T(128)S(6)} %select_n.29), kind=kOutput, calls=%fused_computation.clone.1 | convolution fusion | flops 453427200 | bytes 6684677 | tf_op jit(solution)/shard_map/while/body/eval_jaxpr/dot_general | solution.py:55
  160.2 0.9 constant_dynamic-slice_fusion.3
  161.5 2.6 %convolution_add_fusion.2 = f32[2304,96]{0,1:T(8,128)S(1)} fusion(bf16[2304,1024]{1,0:T(8,128)(2,1)S(1)} %bitcast.16, f32[2304,96]{0,1:T(8,128)S(1)} %get-tuple-element.179, pred[]{:T(512)S(6)} %compare.3, bf16[96,16384]{1,0:T(8,128)(2,1)} %get-tuple-element.191, s32[]{:T(128)S(6)} %select_n.29), kind=kOutput, calls=%fused_computation.clone.1 | convolution fusion | flops 453427200 | bytes 6684677 | tf_op jit(solution)/shard_map/while/body/eval_jaxpr/dot_general | solution.py:55
  164.1 1.4 copy.12
  165.5 3.6 %all-to-all-start = ((f32[4,6,2,24,2,96]{5,4,3,2,1,0:T(2,128)}), f32[4,6,2,24,2,96]{5,4,3,2,1,0:T(2,128)S(1)}, u32[]{:S(2)}, u32[]{:S(2)}) async-start(f32[4,6,2,24,2,96]{5,4,3,2,1,0:T(2,128)} %bitcast.2), calls=%async_computation | async-start | bytes 2359296 | tf_op jit(solution)/shard_map/all_to_all | solution.py:40
  169.4 14.6 %all-to-all-done = f32[4,6,2,24,2,96]{5,4,3,2,1,0:T(2,128)S(1)} async-done(((f32[4,6,2,24,2,96]{5,4,3,2,1,0:T(2,128)}), f32[4,6,2,24,2,96]{5,4,3,2,1,0:T(2,128)S(1)}, u32[]{:S(2)}, u32[]{:S(2)}) %all-to-all-start) | async-done | bytes 884768 | tf_op jit(solution)/shard_map/all_to_all | solution.py:40
  184.9 0.9 fusion.4
  (40 shorter events, 9.1 us)
Async XLA Ops:
  0.0 1.4 copy-start.1
  7.9 42.2 %collective-permute-start.2 = (bf16[48,16384]{1,0:T(8,128)(2,1)}, bf16[48,16384]{1,0:T(8,128)(2,1)}, u32[]{:S(2)}, u32[]{:S(2)}) collective-permute-start(bf16[48,16384]{1,0:T(8,128)(2,1)} %reshape.65), channel_id=1, source_target_pairs={{0,248},{8,0},{16,8},{24,16},{32,24},{40,32},{48,40},{56,48},{64,5... | collective-permute-start | bytes 4718600 | tf_op jit(solution)/shard_map/ppermute | solution.py:12
  16.8 38.9 %collective-permute-start = (bf16[48,16384]{1,0:T(8,128)(2,1)}, bf16[48,16384]{1,0:T(8,128)(2,1)}, u32[]{:S(2)}, u32[]{:S(2)}) collective-permute-start(bf16[48,16384]{1,0:T(8,128)(2,1)} %reshape.65), channel_id=1, source_target_pairs={{0,8},{8,16},{16,24},{24,32},{32,40},{40,48},{48,56},{56,64},{64,7... | collective-permute-start | bytes 4718600 | tf_op jit(solution)/shard_map/ppermute | solution.py:12
  50.2 38.0 %collective-permute-start.3 = (bf16[48,16384]{1,0:T(8,128)(2,1)}, bf16[48,16384]{1,0:T(8,128)(2,1)S(1)}, u32[]{:S(2)}, u32[]{:S(2)}) collective-permute-start(bf16[48,16384]{1,0:T(8,128)(2,1)} %collective-permute-done.2), channel_id=1, source_target_pairs={{0,248},{8,0},{16,8},{24,16},{32,24},{40,32},{48,40},{56,48},{64,5... | collective-permute-start | bytes 4718600 | tf_op jit(solution)/shard_map/ppermute | solution.py:12
  55.7 37.6 %collective-permute-start.1 = (bf16[48,16384]{1,0:T(8,128)(2,1)}, bf16[48,16384]{1,0:T(8,128)(2,1)S(1)}, u32[]{:S(2)}, u32[]{:S(2)}) collective-permute-start(bf16[48,16384]{1,0:T(8,128)(2,1)} %collective-permute-done), channel_id=1, source_target_pairs={{0,8},{8,16},{16,24},{24,32},{32,40},{40,48},{48,56},{56,64},{64,7... | collective-permute-start | bytes 4718600 | tf_op jit(solution)/shard_map/ppermute | solution.py:12
  88.2 1.7 copy-start
  96.0 69.4 %all-to-all-start.1 = ((f32[4,1,192]{2,1,0:T(1,128)}), f32[4,1,192]{2,1,0:T(1,128)S(1)}, u32[]{:S(2)}, u32[]{:S(2)}) async-start(f32[4,1,192]{2,1,0:T(1,128)} %broadcast_in_dim.16), calls=%async_computation.1 | async-start | bytes 8192 | tf_op jit(solution)/shard_map/all_to_all | solution.py:17
  165.5 18.6 %all-to-all-start = ((f32[4,6,2,24,2,96]{5,4,3,2,1,0:T(2,128)}), f32[4,6,2,24,2,96]{5,4,3,2,1,0:T(2,128)S(1)}, u32[]{:S(2)}, u32[]{:S(2)}) async-start(f32[4,6,2,24,2,96]{5,4,3,2,1,0:T(2,128)} %bitcast.2), calls=%async_computation | async-start | bytes 2359296 | tf_op jit(solution)/shard_map/all_to_all | solution.py:40
where the time goes:
time: 187 us; the launch traced here: 186 us
  waiting for transfers between devices  81.7 us (44%)
  matrix products  41.9 us (22%)
  local copies, waits for them, and re-layouts  26.2 us (14%)
  starting transfers between devices  23.9 us (13%)
  other arithmetic  11.4 us (6%)
    ppermute x4, waiting for transfers between devices, passed_along(): lax.ppermute(value, axis, [(i, (i + by) % count) for i in range(count)])  67.1 us
    dot_general x16, matrix products, add_block(): lax.dot_general(pair_rows, partner_cut, (((1,), (1,)), ((), ())), preferr...  41.9 us
    all_to_all x1, waiting for transfers between devices, sum_at_owner(): lax.all_to_all(blocks, axis, split_axis=0, concat_axis=0, tiled=True)  14.6 us
    dynamic_slice x16, local copies, waits for them, and re-layouts, add_block(): third_cut = lax.dynamic_slice_in_dim(third_rows, offset, block_width, 1)  14.6 us
    ppermute x4, starting transfers between devices, passed_along(): lax.ppermute(value, axis, [(i, (i + by) % count) for i in range(count)])  14.4 us
    all_to_all x1, starting transfers between devices, sent_to_all(): return lax.all_to_all(copies, axis, split_axis=0, concat_axis=0, tiled=True)  5.96 us
    mul x16, other arithmetic, add_block(): first_cut[:, None, :] * third_cut[None, :, :]  4.95 us
  transfers between devices with their start and end apart: 6, of which 4 were waited for; matrix products, arithmetic and copies ran while one was open for 35% of the time, Pallas kernels for 0%

commit v1 on v0

v1 whole, which is shorter than its diff:
```python
import jax
import jax.numpy as jnp
from jax import lax
from jax.experimental import pallas as pl
from jax.experimental.pallas import tpu as pltpu
from jax.sharding import PartitionSpec as P

F = 65536
VB = 24
N_VEC = 32
N_FIELD = 4
N_REP = 2
SHARE = VB // N_FIELD
CHUNKS = 2
STEP = 1024
PAIRS = VB * 2 * VB
ROWS = PAIRS + 96
COLS = 64
PACKED = 96


def shifted(value, by):
    return lax.ppermute(value, "vec", [(i, (i + by) % N_VEC) for i in range(N_VEC)])


def fill_and_multiply(u_ref, a1_ref, a2_ref, b1_ref, b2_ref, lhs_ref):
    width = u_ref.shape[1]
    own = u_ref[...]
    third = jnp.concatenate([a1_ref[...], a2_ref[...]], axis=0)
    for i in range(VB):
        lhs_ref[i * 48 : (i + 1) * 48, :] = own[i : i + 1, :] * third
    ones = jnp.ones((VB, width), jnp.bfloat16)
    lhs_ref[PAIRS:, :] = jnp.concatenate([third, own, ones], axis=0)
    partner = jnp.concatenate([b1_ref[...], b2_ref[...], ones[:16]], axis=0)
    return lax.dot_general(
        lhs_ref[...], partner, (((1,), (1,)), ((), ())), preferred_element_type=jnp.float32
    )


def pack(acc_ref, out_ref):
    for q in range(N_FIELD):
        singles = jnp.concatenate(
            [
                acc_ref[PAIRS + 72 : PAIRS + 73, :],
                acc_ref[PAIRS + 48 + SHARE * q : PAIRS + 48 + SHARE * (q + 1), :],
                jnp.zeros((1, COLS), jnp.float32),
            ],
            axis=0,
        )
        for r in range(N_REP):
            dest = r * N_FIELD + q
            for ii in range(3):
                for half in range(2):
                    row = (SHARE * q + 3 * half + ii) * 48 + VB * r
                    out_ref[dest, ii * VB : (ii + 1) * VB, half * COLS : (half + 1) * COLS] = acc_ref[
                        row : row + VB, :
                    ]
            out_ref[dest, 72:96, :COLS] = acc_ref[PAIRS + VB * r : PAIRS + VB * (r + 1), :]
            out_ref[dest, 72:80, COLS:] = singles
            out_ref[dest, 80:96, COLS:] = jnp.zeros((16, COLS), jnp.float32)


def first_kernel(u_ref, a1_ref, a2_ref, b1_ref, b2_ref, acc_ref, lhs_ref):
    product = fill_and_multiply(u_ref, a1_ref, a2_ref, b1_ref, b2_ref, lhs_ref)

    @pl.when(pl.program_id(0) == 0)
    def _():
        acc_ref[...] = product

    @pl.when(pl.program_id(0) > 0)
    def _():
        acc_ref[...] += product


def last_kernel(u_ref, a1_ref, a2_ref, b1_ref, b2_ref, before_ref, out_ref, lhs_ref, acc_ref):
    product = fill_and_multiply(u_ref, a1_ref, a2_ref, b1_ref, b2_ref, lhs_ref)

    @pl.when(pl.program_id(0) == 0)
    def _():
        acc_ref[...] = before_ref[...] + product

    @pl.when(pl.program_id(0) > 0)
    def _():
        acc_ref[...] += product

    @pl.when(pl.program_id(0) == pl.num_programs(0) - 1)
    def _():
        pack(acc_ref, out_ref)


def tables_of(blocks, before):
    width = blocks[0].shape[1]
    steps = width // STEP
    block_spec = pl.BlockSpec((VB, STEP), lambda s: (0, s))
    acc_spec = pl.BlockSpec((ROWS, COLS), lambda s: (0, 0))
    cost = pl.CostEstimate(
        flops=2 * ROWS * width * 256, bytes_accessed=5 * VB * width * 2, transcendentals=0
    )
    params = pltpu.CompilerParams(vmem_limit_bytes=32 * 2**20)
    lhs = pltpu.VMEM((ROWS, STEP), jnp.bfloat16)
    if before is None:
        return pl.pallas_call(
            first_kernel,
            grid=(steps,),
            in_specs=[block_spec] * 5,
            out_specs=acc_spec,
            out_shape=jax.ShapeDtypeStruct((ROWS, COLS), jnp.float32),
            scratch_shapes=[lhs],
            compiler_params=params,
            cost_estimate=cost,
            name="tables_first",
        )(*blocks)
    return pl.pallas_call(
        last_kernel,
        grid=(steps,),
        in_specs=[block_spec] * 5 + [acc_spec],
        out_specs=pl.BlockSpec((8, PACKED, 128), lambda s: (0, 0, 0)),
        out_shape=jax.ShapeDtypeStruct((8, PACKED, 128), jnp.float32),
        scratch_shapes=[lhs, pltpu.VMEM((ROWS, COLS), jnp.float32)],
        compiler_params=params,
        cost_estimate=cost,
        name="tables_last",
    )(*blocks, before)


def finish_kernel(parts_ref, out_ref):
    summed = jnp.sum(parts_ref[...], axis=0)
    row = lax.broadcasted_iota(jnp.int32, (128, 256), 0)
    col = lax.broadcasted_iota(jnp.int32, (128, 256), 1)
    same_half = (row >= COLS) == (col >= 128)
    lane = jnp.where(row >= COLS, row - COLS, row)
    target = jnp.where(col >= 128, col - 128, col)
    even = (target % 2) == 0
    inside = same_half & (target < 96)
    entry = jnp.where(inside & (target // 2 == lane), jnp.where(even, -1.0, 1.0), 0.0)
    entry = entry + jnp.where(inside & even & (lane == 48), 2.0, 0.0)
    spread = jnp.dot(
        summed, entry, precision=lax.Precision.HIGHEST, preferred_element_type=jnp.float32
    )
    third_row = spread[72:96, :96]
    singles = spread[72:80, 128:224]
    ones_row = singles[0:1]

    def gain(total):
        return 1.0 - total / (3.0 * F)

    gain_partner = gain(ones_row) * (4.5 / (8.0 * F))
    third_total = summed[72:96, 48:49]
    own_total = summed[72:80, 112:113]
    third_gain = (gain(2.0 * F - third_total), gain(third_total))
    own_gain = (gain(2.0 * F - own_total), gain(own_total))
    for i in range(SHARE):
        half, ii = divmod(i, 3)
        pair = spread[ii * VB : (ii + 1) * VB, half * 128 : half * 128 + 96]
        own_row = singles[1 + i : 2 + i]
        by_place = {
            (1, 1): pair,
            (1, 0): 2.0 * own_row - pair,
            (0, 1): 2.0 * third_row - pair,
            (0, 0): (4.0 * ones_row - 2.0 * own_row) - (2.0 * third_row - pair),
        }
        for a in range(2):
            partner = gain_partner * own_gain[a][1 + i : 2 + i]
            for c in range(2):
                out_ref[i, a, pl.ds(c, VB, stride=2), :] = by_place[a, c] * third_gain[c] * partner


def finish(parts):
    return pl.pallas_call(
        finish_kernel,
        out_shape=jax.ShapeDtypeStruct((SHARE, 2, 2 * VB, 96), jnp.float32),
        name="finish",
    )(parts)


def body(dosage):
    rep_plane = lax.axis_index("rep")
    width = dosage.shape[1] // N_REP // CHUNKS
    own = [
        lax.dynamic_slice_in_dim(dosage, (rep_plane * CHUNKS + n) * width, width, 1)
        for n in range(CHUNKS)
    ]
    near = [(shifted(u, 1), shifted(u, -1)) for u in own]
    far = [(shifted(a, 1), shifted(b, -1)) for a, b in near]
    state = None
    for u, (a1, b1), (a2, b2) in zip(own, near, far):
        state = tables_of((u, a1, a2, b1, b2), state)
    parts = lax.all_to_all(state, ("rep", "field"), split_axis=0, concat_axis=0, tiled=True)
    return finish(parts).reshape(1, SHARE, 2, VB, 2, 96)


def solution(mesh):
    return jax.shard_map(
        body,
        mesh=mesh,
        in_specs=(P("vec", "field"),),
        out_specs=P("rep", ("vec", "field"), None, None, None, None),
        check_vma=False,
    )
```

time: 187 us -> 54.2 us (0.29)
  waiting for transfers between devices: 81.7 us -> 4.21 us
  matrix products: 41.9 us -> 0 us
  local copies, waits for them, and re-layouts: 26.2 us -> 1.05 us
  blocking collectives: 0 us -> 16.1 us
  other arithmetic: 11.4 us -> 0 us
  Pallas kernels: 0 us -> 9.4 us
    ppermute x4 -> x8, waiting for transfers between devices: 67.1 us -> 4.21 us  [shifted(): lax.ppermute(value, 'vec', [(i, (i + by) % N_VEC) for i in range(N_VEC)])]
    dot_general x16 -> x0, matrix products: 41.9 us -> none  [add_block(): lax.dot_general(pair_rows, partner_cut, (((1,), (1,)), ((), ())), preferr...]
    all_to_all x0 -> x1, blocking collectives: none -> 16.1 us  [body(): lax.all_to_all(state, ('rep', 'field'), split_axis=0, concat_axis=0, tile...]
    all_to_all x2 -> x0, waiting for transfers between devices: 14.6 us -> none  [the longest x1 14.6 us: sum_at_owner(): lax.all_to_all(blocks, axis, split_axis=0, concat_axis=0, tiled=True)]
    dynamic_slice x16 -> x1, local copies, waits for them, and re-layouts: 14.6 us -> 1.05 us  [body(): lax.dynamic_slice_in_dim(dosage, (rep_plane * CHUNKS + n) * width, width, 1)]
    all_to_all x2 -> x0, starting transfers between devices: 9.52 us -> none  [the longest x1 5.96 us: sent_to_all(): return lax.all_to_all(copies, axis, split_axis=0, concat_axis=0, tiled=True)]
    pallas_call x0 -> x3, Pallas kernels: none -> 9.4 us  [the longest x1 3.81 us: tables_of(): pl.pallas_call(last_kernel, grid=(steps,), in_specs=[block_spec] * 5 + [a...]
    ppermute x4 -> x8, starting transfers between devices: 14.4 us -> 23.3 us  [shifted(): lax.ppermute(value, 'vec', [(i, (i + by) % N_VEC) for i in range(N_VEC)])]
  transfers between devices with their start and end apart: 6 -> 8, of which waited for: 4 -> 2; matrix products, arithmetic and copies ran while one was open for 35% -> 0% of each run, Pallas kernels for 0% -> 7%
where the time goes in v1:
time: 54.2 us; the launch traced here: 54.1 us
  starting transfers between devices  23.3 us (43%)
  blocking collectives  16.1 us (30%)
  Pallas kernels  9.4 us (17%)
  waiting for transfers between devices  4.21 us (8%)
  local copies, waits for them, and re-layouts  1.05 us (2%)
    ppermute x8, starting transfers between devices, shifted(): lax.ppermute(value, 'vec', [(i, (i + by) % N_VEC) for i in range(N_VEC)])  23.3 us
    all_to_all x1, blocking collectives, body(): lax.all_to_all(state, ('rep', 'field'), split_axis=0, concat_axis=0, tile...  16.1 us
    ppermute x8, waiting for transfers between devices, shifted(): lax.ppermute(value, 'vec', [(i, (i + by) % N_VEC) for i in range(N_VEC)])  4.21 us
    pallas_call x1, Pallas kernels, tables_of(): pl.pallas_call(last_kernel, grid=(steps,), in_specs=[block_spec] * 5 + [a...  3.81 us
    pallas_call x1, Pallas kernels, tables_of(): pl.pallas_call(first_kernel, grid=(steps,), in_specs=[block_spec] * 5, ou...  3.62 us
    pallas_call x1, Pallas kernels, finish(): pl.pallas_call(finish_kernel, out_shape=jax.ShapeDtypeStruct((SHARE, 2, 2...  1.98 us
  transfers between devices with their start and end apart: 8, of which 2 were waited for; matrix products, arithmetic and copies ran while one was open for 0% of the time, Pallas kernels for 7%

profile of v1, /device:TPU:1, one launch (start us, length us, event | category | flops | bytes accessed | tf_op | source)
XLA Modules:
  0.0 54.1 jit_solution(2036184056172063082)
XLA Ops:
  0.0 1.0 %constant_dynamic-slice_fusion = (bf16[24,4096]{1,0:T(8,128)(2,1)S(1)}, bf16[24,4096]{1,0:T(8,128)(2,1)S(1)}) fusion(bf16[24,16384]{1,0:T(8,128)(2,1)} %param.1, s32[]{:T(128)S(6)} %select_n.7, s32[]{:T(128)S(6)} %select_n.6), kind=kLoop, calls=%fused_computation | loop fusion | bytes 786440 | tf_op jit(solution)/shard_map/dynamic_slice | solution.py:180
  1.1 8.9 %collective-permute-start.6 = (bf16[24,4096]{1,0:T(8,128)(2,1)S(1)}, bf16[24,4096]{1,0:T(8,128)(2,1)S(1)}, u32[]{:S(2)}, u32[]{:S(2)}) collective-permute-start(bf16[24,4096]{1,0:T(8,128)(2,1)S(1)} %get-tuple-element.5.u_ref), channel_id=1, source_target_pairs={{0,248},{8,0},{16,8},{24,16},{32,24},{40,32},{48,40},{56,48},{64,5... | collective-permute-start | bytes 589832 | tf_op jit(solution)/shard_map/ppermute | solution.py:23
  10.0 0.0 collective-permute-start.4
  10.0 4.8 %collective-permute-start.2 = (bf16[24,4096]{1,0:T(8,128)(2,1)S(1)}, bf16[24,4096]{1,0:T(8,128)(2,1)S(1)}, u32[]{:S(2)}, u32[]{:S(2)}) collective-permute-start(bf16[24,4096]{1,0:T(8,128)(2,1)S(1)} %get-tuple-element.6.u_ref), channel_id=1, source_target_pairs={{0,248},{8,0},{16,8},{24,16},{32,24},{40,32},{48,40},{56,48},{64,5... | collective-permute-start | bytes 589832 | tf_op jit(solution)/shard_map/ppermute | solution.py:23
  14.8 0.0 collective-permute-start
  14.8 0.0 collective-permute-done.6.b1_ref
  14.8 4.8 %collective-permute-start.7 = (bf16[24,4096]{1,0:T(8,128)(2,1)S(1)}, bf16[24,4096]{1,0:T(8,128)(2,1)S(1)}, u32[]{:S(2)}, u32[]{:S(2)}) collective-permute-start(bf16[24,4096]{1,0:T(8,128)(2,1)S(1)} %collective-permute-done.6.b1_ref), channel_id=1, source_target_pairs={{0,248},{8,0},{16,8},{24,16},{32,24},{40,32},{48,40},{56,48},{64,5... | collective-permute-start | bytes 589832 | tf_op jit(solution)/shard_map/ppermute | solution.py:23
  19.6 0.0 collective-permute-done.4.a1_ref
  19.6 0.0 collective-permute-start.5
  19.6 0.0 collective-permute-done.2.b1_ref
  19.6 4.8 %collective-permute-start.3 = (bf16[24,4096]{1,0:T(8,128)(2,1)S(1)}, bf16[24,4096]{1,0:T(8,128)(2,1)S(1)}, u32[]{:S(2)}, u32[]{:S(2)}) collective-permute-start(bf16[24,4096]{1,0:T(8,128)(2,1)S(1)} %collective-permute-done.2.b1_ref), channel_id=1, source_target_pairs={{0,248},{8,0},{16,8},{24,16},{32,24},{40,32},{48,40},{56,48},{64,5... | collective-permute-start | bytes 589832 | tf_op jit(solution)/shard_map/ppermute | solution.py:23
  24.4 0.0 collective-permute-done.a1_ref
  24.4 0.0 collective-permute-start.1
  24.4 0.0 collective-permute-done.7.b2_ref
  24.4 3.0 %collective-permute-done.5.a2_ref = bf16[24,4096]{1,0:T(8,128)(2,1)S(1)} collective-permute-done((bf16[24,4096]{1,0:T(8,128)(2,1)S(1)}, bf16[24,4096]{1,0:T(8,128)(2,1)S(1)}, u32[]{:S(2)}, u32[]{:S(2)}) %collective-permute-start.5) | collective-permute-done | bytes 196640 | tf_op jit(solution)/shard_map/ppermute | solution.py:23
  27.4 3.6 %tables_first.1.before_ref = f32[1248,64]{1,0:T(8,128)S(1)} custom-call(bf16[24,4096]{1,0:T(8,128)(2,1)S(1)} %get-tuple-element.5.u_ref, bf16[24,4096]{1,0:T(8,128)(2,1)S(1)} %collective-permute-done.4.a1_ref, bf16[24,4096]{1,0:T(8,128)(2,1)S(1)} %collective-permute-done.5.a2_ref, bf16[24,4096]{1,0:T(8,128)(2,1)S(1)} %collective-permute-done.6.b1_ref, ...), custom_call_target="tpu_custom_call" | custom-call | flops 2617245696 | bytes 983040 | tf_op jit(solution)/shard_map/tables_first/pallas_call | solution.py:102
  31.0 0.0 collective-permute-done.3.b2_ref
  31.0 1.2 %collective-permute-done.1.a2_ref = bf16[24,4096]{1,0:T(8,128)(2,1)S(1)} collective-permute-done((bf16[24,4096]{1,0:T(8,128)(2,1)S(1)}, bf16[24,4096]{1,0:T(8,128)(2,1)S(1)}, u32[]{:S(2)}, u32[]{:S(2)}) %collective-permute-start.1) | collective-permute-done | bytes 196640 | tf_op jit(solution)/shard_map/ppermute | solution.py:23
  32.2 3.8 %tables_last.1 = f32[8,96,128]{2,1,0:T(8,128)S(1)} custom-call(bf16[24,4096]{1,0:T(8,128)(2,1)S(1)} %get-tuple-element.6.u_ref, bf16[24,4096]{1,0:T(8,128)(2,1)S(1)} %collective-permute-done.a1_ref, bf16[24,4096]{1,0:T(8,128)(2,1)S(1)} %collective-permute-done.1.a2_ref, bf16[24,4096]{1,0:T(8,128)(2,1)S(1)} %collective-permute-done.2.b1_ref, ...), custom_call_target="tpu_custom_call" | custom-call | flops 2617245696 | bytes 983040 | tf_op jit(solution)/shard_map/tables_last/pallas_call | solution.py:113
  36.0 16.1 %all_to_all.5.parts_ref = f32[8,96,128]{2,1,0:T(8,128)} all-to-all(f32[8,96,128]{2,1,0:T(8,128)S(1)} %tables_last.1), channel_id=1, replica_groups=mesh['vec'=32,'field'=4,'rep'=2] {'rep','field'}, dimensions={0} | all-to-all | bytes 786432 | tf_op jit(solution)/shard_map/all_to_all | solution.py:188
  52.1 2.0 %finish.1 = f32[6,2,48,96]{3,2,1,0:T(8,128)} custom-call(f32[8,96,128]{2,1,0:T(8,128)} %all_to_all.5.parts_ref), custom_call_target="tpu_custom_call" | custom-call | tf_op jit(solution)/shard_map/finish/pallas_call | solution.py:169
Async XLA Ops:
  1.1 13.7 %collective-permute-start.6 = (bf16[24,4096]{1,0:T(8,128)(2,1)S(1)}, bf16[24,4096]{1,0:T(8,128)(2,1)S(1)}, u32[]{:S(2)}, u32[]{:S(2)}) collective-permute-start(bf16[24,4096]{1,0:T(8,128)(2,1)S(1)} %get-tuple-element.5.u_ref), channel_id=1, source_target_pairs={{0,248},{8,0},{16,8},{24,16},{32,24},{40,32},{48,40},{56,48},{64,5... | collective-permute-start | bytes 589832 | tf_op jit(solution)/shard_map/ppermute | solution.py:23
  10.0 9.6 %collective-permute-start.4 = (bf16[24,4096]{1,0:T(8,128)(2,1)S(1)}, bf16[24,4096]{1,0:T(8,128)(2,1)S(1)}, u32[]{:S(2)}, u32[]{:S(2)}) collective-permute-start(bf16[24,4096]{1,0:T(8,128)(2,1)S(1)} %get-tuple-element.5.u_ref), channel_id=1, source_target_pairs={{0,8},{8,16},{16,24},{24,32},{32,40},{40,48},{48,56},{56,64},{64,7... | collective-permute-start | bytes 589832 | tf_op jit(solution)/shard_map/ppermute | solution.py:23
  10.0 9.6 %collective-permute-start.2 = (bf16[24,4096]{1,0:T(8,128)(2,1)S(1)}, bf16[24,4096]{1,0:T(8,128)(2,1)S(1)}, u32[]{:S(2)}, u32[]{:S(2)}) collective-permute-start(bf16[24,4096]{1,0:T(8,128)(2,1)S(1)} %get-tuple-element.6.u_ref), channel_id=1, source_target_pairs={{0,248},{8,0},{16,8},{24,16},{32,24},{40,32},{48,40},{56,48},{64,5... | collective-permute-start | bytes 589832 | tf_op jit(solution)/shard_map/ppermute | solution.py:23
  14.8 9.6 %collective-permute-start = (bf16[24,4096]{1,0:T(8,128)(2,1)S(1)}, bf16[24,4096]{1,0:T(8,128)(2,1)S(1)}, u32[]{:S(2)}, u32[]{:S(2)}) collective-permute-start(bf16[24,4096]{1,0:T(8,128)(2,1)S(1)} %get-tuple-element.6.u_ref), channel_id=1, source_target_pairs={{0,8},{8,16},{16,24},{24,32},{32,40},{40,48},{48,56},{56,64},{64,7... | collective-permute-start | bytes 589832 | tf_op jit(solution)/shard_map/ppermute | solution.py:23
  14.8 9.6 %collective-permute-start.7 = (bf16[24,4096]{1,0:T(8,128)(2,1)S(1)}, bf16[24,4096]{1,0:T(8,128)(2,1)S(1)}, u32[]{:S(2)}, u32[]{:S(2)}) collective-permute-start(bf16[24,4096]{1,0:T(8,128)(2,1)S(1)} %collective-permute-done.6.b1_ref), channel_id=1, source_target_pairs={{0,248},{8,0},{16,8},{24,16},{32,24},{40,32},{48,40},{56,48},{64,5... | collective-permute-start | bytes 589832 | tf_op jit(solution)/shard_map/ppermute | solution.py:23
  19.6 7.8 %collective-permute-start.5 = (bf16[24,4096]{1,0:T(8,128)(2,1)S(1)}, bf16[24,4096]{1,0:T(8,128)(2,1)S(1)}, u32[]{:S(2)}, u32[]{:S(2)}) collective-permute-start(bf16[24,4096]{1,0:T(8,128)(2,1)S(1)} %collective-permute-done.4.a1_ref), channel_id=1, source_target_pairs={{0,8},{8,16},{16,24},{24,32},{32,40},{40,48},{48,56},{56,64},{64,7... | collective-permute-start | bytes 589832 | tf_op jit(solution)/shard_map/ppermute | solution.py:23
  19.6 11.5 %collective-permute-start.3 = (bf16[24,4096]{1,0:T(8,128)(2,1)S(1)}, bf16[24,4096]{1,0:T(8,128)(2,1)S(1)}, u32[]{:S(2)}, u32[]{:S(2)}) collective-permute-start(bf16[24,4096]{1,0:T(8,128)(2,1)S(1)} %collective-permute-done.2.b1_ref), channel_id=1, source_target_pairs={{0,248},{8,0},{16,8},{24,16},{32,24},{40,32},{48,40},{56,48},{64,5... | collective-permute-start | bytes 589832 | tf_op jit(solution)/shard_map/ppermute | solution.py:23
  24.4 7.8 %collective-permute-start.1 = (bf16[24,4096]{1,0:T(8,128)(2,1)S(1)}, bf16[24,4096]{1,0:T(8,128)(2,1)S(1)}, u32[]{:S(2)}, u32[]{:S(2)}) collective-permute-start(bf16[24,4096]{1,0:T(8,128)(2,1)S(1)} %collective-permute-done.a1_ref), channel_id=1, source_target_pairs={{0,8},{8,16},{16,24},{24,32},{32,40},{40,48},{48,56},{56,64},{64,7... | collective-permute-start | bytes 589832 | tf_op jit(solution)/shard_map/ppermute | solution.py:23

commit v2 on v1

v2 whole, which is shorter than its diff:
```python
import jax
import jax.numpy as jnp
from jax import lax
from jax.experimental import pallas as pl
from jax.experimental.pallas import tpu as pltpu
from jax.sharding import Mesh, PartitionSpec as P

F = 65536
VB = 24
N_VEC = 32
SHARE = 6
WIDTHS = (4096, 4096)
STEP = 1024
PAIRS = VB * 2 * VB
ROWS = PAIRS + 96
COLS = 64
PACKED = 96
SWAP = ((0, 1), (1, 0))


def swapped(value, odd):
    pairs = [(i, (((i + odd) ^ 1) - odd) % N_VEC) for i in range(N_VEC)]
    return lax.ppermute(value, "vec", pairs)


def to_chip(value, flip):
    return lax.ppermute(value, ("xlo", "rep"), [(i, i ^ flip) for i in range(4)])


def accumulate(u_ref, third_refs, partner_refs, lhs_ref, acc_ref, start):
    width = u_ref.shape[1]
    for at in range(0, width, STEP):
        step = min(STEP, width - at)
        cut = slice(at, at + step)
        own = u_ref[:, cut]
        third = jnp.concatenate([ref[:, cut] for ref in third_refs], axis=0)
        for i in range(VB):
            lhs_ref[i * 48 : (i + 1) * 48, :step] = own[i : i + 1, :] * third
        ones = jnp.ones((VB, step), jnp.bfloat16)
        lhs_ref[PAIRS:, :step] = jnp.concatenate([third, own, ones], axis=0)
        partner = jnp.concatenate([ref[:, cut] for ref in partner_refs] + [ones[:16]], axis=0)
        product = lax.dot_general(
            lhs_ref[:, :step], partner, (((1,), (1,)), ((), ())), preferred_element_type=jnp.float32
        )
        if at > 0:
            acc_ref[...] += product
        elif start is None:
            acc_ref[...] = product
        else:
            acc_ref[...] = start[...] + product


def pack(acc_ref, out_ref):
    for core in range(2):
        for chip in range(4):
            xlo, rep = divmod(chip, 2)
            q = xlo * 2 + core
            for ii in range(3):
                for half in range(2):
                    row = (SHARE * q + 3 * half + ii) * 48 + VB * rep
                    out_ref[core, chip, ii * VB : (ii + 1) * VB, half * COLS : (half + 1) * COLS] = (
                        acc_ref[row : row + VB, :]
                    )
            out_ref[core, chip, 72:96, :COLS] = acc_ref[PAIRS + VB * rep : PAIRS + VB * (rep + 1), :]
            out_ref[core, chip, 72:80, COLS:] = jnp.concatenate(
                [
                    acc_ref[PAIRS + 72 : PAIRS + 73, :],
                    acc_ref[PAIRS + 48 + SHARE * q : PAIRS + 48 + SHARE * (q + 1), :],
                    jnp.zeros((1, COLS), jnp.float32),
                ],
                axis=0,
            )
            out_ref[core, chip, 80:96, COLS:] = jnp.zeros((16, COLS), jnp.float32)


def tables_kernel(u_ref, a1_ref, a2_ref, b1_ref, b2_ref, *rest, first, last):
    start = None if first else rest[0]
    out_ref, lhs_ref = rest[-3 if last else -2], rest[-2 if last else -1]
    acc_ref = rest[-1] if last else out_ref
    accumulate(u_ref, (a1_ref, a2_ref), (b1_ref, b2_ref), lhs_ref, acc_ref, start)
    if last:
        pack(acc_ref, out_ref)


def tables_of(blocks, before, last):
    width = blocks[0].shape[1]
    first = before is None
    shape = (2, 4, PACKED, 128) if last else (ROWS, COLS)
    scratch = [pltpu.VMEM((ROWS, STEP), jnp.bfloat16)]
    if last:
        scratch.append(pltpu.VMEM((ROWS, COLS), jnp.float32))

    def kernel(*refs):
        tables_kernel(*refs, first=first, last=last)

    return pl.pallas_call(
        kernel,
        out_shape=jax.ShapeDtypeStruct(shape, jnp.float32),
        scratch_shapes=scratch,
        compiler_params=pltpu.CompilerParams(vmem_limit_bytes=32 * 2**20),
        cost_estimate=pl.CostEstimate(
            flops=2 * ROWS * width * 256, bytes_accessed=5 * VB * width * 2, transcendentals=0
        ),
        name="tables",
    )(*blocks, *(() if first else (before,)))


def finish_kernel(own_ref, one_ref, two_ref, three_ref, out_ref):
    summed = (own_ref[0] + one_ref[...]) + (two_ref[...] + three_ref[...])
    row = lax.broadcasted_iota(jnp.int32, (128, 256), 0)
    col = lax.broadcasted_iota(jnp.int32, (128, 256), 1)
    same_half = (row >= COLS) == (col >= 128)
    lane = jnp.where(row >= COLS, row - COLS, row)
    target = jnp.where(col >= 128, col - 128, col)
    even = (target % 2) == 0
    inside = same_half & (target < 96)
    entry = jnp.where(inside & (target // 2 == lane), jnp.where(even, -1.0, 1.0), 0.0)
    entry = entry + jnp.where(inside & even & (lane == 48), 2.0, 0.0)
    spread = jnp.dot(
        summed, entry, precision=lax.Precision.HIGHEST, preferred_element_type=jnp.float32
    )
    third_row = spread[72:96, :96]
    singles = spread[72:80, 128:224]
    ones_row = singles[0:1]

    def gain(total):
        return 1.0 - total / (3.0 * F)

    gain_partner = gain(ones_row) * (4.5 / (8.0 * F))
    third_total = summed[72:96, 48:49]
    own_total = summed[72:80, 112:113]
    third_gain = (gain(2.0 * F - third_total), gain(third_total))
    own_gain = (gain(2.0 * F - own_total), gain(own_total))
    for i in range(SHARE):
        half, ii = divmod(i, 3)
        pair = spread[ii * VB : (ii + 1) * VB, half * 128 : half * 128 + 96]
        own_row = singles[1 + i : 2 + i]
        by_place = {
            (1, 1): pair,
            (1, 0): 2.0 * own_row - pair,
            (0, 1): 2.0 * third_row - pair,
            (0, 0): (4.0 * ones_row - 2.0 * own_row) - (2.0 * third_row - pair),
        }
        for a in range(2):
            partner = gain_partner * own_gain[a][1 + i : 2 + i]
            for c in range(2):
                out_ref[i, a, pl.ds(c, VB, stride=2), :] = by_place[a, c] * third_gain[c] * partner


def finish(parts):
    return pl.pallas_call(
        finish_kernel,
        out_shape=jax.ShapeDtypeStruct((SHARE, 2, 2 * VB, 96), jnp.float32),
        name="finish",
    )(*parts)


def body(dosage):
    rep = lax.axis_index("rep")
    core = lax.axis_index("core")
    chip = lax.axis_index("xlo") * 2 + rep
    even = lax.axis_index("vec") % 2 == 0
    half = dosage.shape[1] // 2
    own, at = [], 0
    for width in WIDTHS:
        own.append(lax.dynamic_slice_in_dim(dosage, rep * half + at, width, 1))
        at += width
    near = [(swapped(u, 0), swapped(u, 1)) for u in own]
    far = [(swapped(o, 0), swapped(e, 1)) for e, o in near]
    near = [(jnp.where(even, o, e), jnp.where(even, e, o)) for e, o in near]
    far = [(jnp.where(even, o, e), jnp.where(even, e, o)) for e, o in far]
    state = None
    for n, (u, (a1, b1), (a2, b2)) in enumerate(zip(own, near, far)):
        state = tables_of((u, a1, a2, b1, b2), state, n == len(WIDTHS) - 1)
    kept = lax.dynamic_index_in_dim(state, core, 0, False)
    sent = lax.dynamic_index_in_dim(state, 1 - core, 0, False)
    kept = kept + lax.ppermute(sent, "core", SWAP)
    parts = [lax.dynamic_slice_in_dim(kept, chip, 1, 0)]
    for flip in (1, 3, 2):
        parts.append(to_chip(lax.dynamic_index_in_dim(kept, chip ^ flip, 0, False), flip))
    return finish(parts).reshape(1, SHARE, 2, VB, 2, 96)


def solution(mesh):
    split = Mesh(mesh.devices.reshape(N_VEC, 2, 2, 2), ("vec", "xlo", "core", "rep"))
    return jax.shard_map(
        body,
        mesh=split,
        in_specs=(P("vec", ("xlo", "core")),),
        out_specs=P("rep", ("vec", "xlo", "core"), None, None, None, None),
        check_vma=False,
    )
```

time: 54.2 us -> 45.6 us (0.84)
  the two profiles are of different devices: /device:TPU:1 before, /device:TPU:2 now
where the time goes in v2:
time: 45.6 us; the launch traced here: 45.5 us
  starting transfers between devices  24.2 us (53%)
  waiting for transfers between devices  10.9 us (24%)
  Pallas kernels  7.79 us (17%)
  local copies, waits for them, and re-layouts  2.31 us (5%)
    ppermute x8, starting transfers between devices, swapped(): return lax.ppermute(value, 'vec', pairs)  20.6 us
    pallas_call x2, Pallas kernels, tables_of(): pl.pallas_call(kernel, out_shape=jax.ShapeDtypeStruct(shape, jnp.float32)...  5.93 us
    ppermute x3, waiting for transfers between devices, to_chip(): lax.ppermute(value, ('xlo', 'rep'), [(i, i ^ flip) for i in range(4)])  5.4 us
    ppermute x8, waiting for transfers between devices, swapped(): return lax.ppermute(value, 'vec', pairs)  4.07 us
    ppermute x3, starting transfers between devices, to_chip(): lax.ppermute(value, ('xlo', 'rep'), [(i, i ^ flip) for i in range(4)])  3.49 us
    pallas_call x1, Pallas kernels, finish(): pl.pallas_call(finish_kernel, out_shape=jax.ShapeDtypeStruct((SHARE, 2, 2...  1.86 us
    ppermute x1, waiting for transfers between devices, body(): kept = kept + lax.ppermute(sent, 'core', SWAP)  1.41 us
    dynamic_slice x1, local copies, waits for them, and re-layouts, body(): own.append(lax.dynamic_slice_in_dim(dosage, rep * half + at, width, 1))  1.05 us
  transfers between devices with their start and end apart: 12, of which 5 were waited for; matrix products, arithmetic and copies ran while one was open for 0% of the time, Pallas kernels for 6%

profile of v2, /device:TPU:2, one launch (start us, length us, event | category | flops | bytes accessed | tf_op | source)
XLA Modules:
  0.0 45.5 jit_solution(5245766211930971765)
XLA Ops:
  0.0 1.0 %constant_dynamic-slice_fusion.1 = (bf16[24,4096]{1,0:T(8,128)(2,1)S(1)}, bf16[24,4096]{1,0:T(8,128)(2,1)S(1)}) fusion(bf16[24,16384]{1,0:T(8,128)(2,1)} %param.1, s32[]{:T(128)S(6)} %select_n.76, s32[]{:T(128)S(6)} %select_n.69), kind=kLoop, calls=%fused_computation.14 | loop fusion | bytes 786440 | tf_op jit(solution)/shard_map/dynamic_slice | solution.py:166
  1.1 2.0 %collective-permute-start.5 = (bf16[24,4096]{1,0:T(8,128)(2,1)S(1)}, bf16[24,4096]{1,0:T(8,128)(2,1)S(1)}, u32[]{:S(2)}, u32[]{:S(2)}) collective-permute-start(bf16[24,4096]{1,0:T(8,128)(2,1)S(1)} %get-tuple-element.5.refs_0_), channel_id=1, source_target_pairs={{0,8},{8,0},{16,24},{24,16},{32,40},{40,32},{48,56},{56,48},{64,72... | collective-permute-start | bytes 589832 | tf_op jit(solution)/shard_map/ppermute | solution.py:23
  3.1 7.4 %collective-permute-start.4 = (bf16[24,4096]{1,0:T(8,128)(2,1)S(1)}, bf16[24,4096]{1,0:T(8,128)(2,1)S(1)}, u32[]{:S(2)}, u32[]{:S(2)}) collective-permute-start(bf16[24,4096]{1,0:T(8,128)(2,1)S(1)} %get-tuple-element.5.refs_0_), channel_id=1, source_target_pairs={{0,248},{8,16},{16,8},{24,32},{32,24},{40,48},{48,40},{56,64},{64,... | collective-permute-start | bytes 589832 | tf_op jit(solution)/shard_map/ppermute | solution.py:23
  10.5 0.0 collective-permute-start.1
  10.5 2.0 %collective-permute-start = (bf16[24,4096]{1,0:T(8,128)(2,1)S(1)}, bf16[24,4096]{1,0:T(8,128)(2,1)S(1)}, u32[]{:S(2)}, u32[]{:S(2)}) collective-permute-start(bf16[24,4096]{1,0:T(8,128)(2,1)S(1)} %get-tuple-element.6.refs_0_), channel_id=1, source_target_pairs={{0,248},{8,16},{16,8},{24,32},{32,24},{40,48},{48,40},{56,64},{64,... | collective-permute-start | bytes 589832 | tf_op jit(solution)/shard_map/ppermute | solution.py:23
  12.5 0.0 collective-permute-done.5
  12.5 4.8 %collective-permute-start.6 = (bf16[24,4096]{1,0:T(8,128)(2,1)S(1)}, bf16[24,4096]{1,0:T(8,128)(2,1)S(1)}, u32[]{:S(2)}, u32[]{:S(2)}) collective-permute-start(bf16[24,4096]{1,0:T(8,128)(2,1)S(1)} %collective-permute-done.5), channel_id=1, source_target_pairs={{0,248},{8,16},{16,8},{24,32},{32,24},{40,48},{48,40},{56,64},{64,... | collective-permute-start | bytes 589832 | tf_op jit(solution)/shard_map/ppermute | solution.py:23
  17.2 0.0 collective-permute-done.4
  17.2 0.0 collective-permute-start.7
  17.3 0.0 collective-permute-done.1
  17.3 4.4 %collective-permute-start.2 = (bf16[24,4096]{1,0:T(8,128)(2,1)S(1)}, bf16[24,4096]{1,0:T(8,128)(2,1)S(1)}, u32[]{:S(2)}, u32[]{:S(2)}) collective-permute-start(bf16[24,4096]{1,0:T(8,128)(2,1)S(1)} %collective-permute-done.1), channel_id=1, source_target_pairs={{0,248},{8,16},{16,8},{24,32},{32,24},{40,48},{48,40},{56,64},{64,... | collective-permute-start | bytes 589832 | tf_op jit(solution)/shard_map/ppermute | solution.py:23
  21.7 0.0 collective-permute-done
  21.7 0.0 collective-permute-start.3
  21.8 4.1 %collective-permute-done.6 = bf16[24,4096]{1,0:T(8,128)(2,1)S(1)} collective-permute-done((bf16[24,4096]{1,0:T(8,128)(2,1)S(1)}, bf16[24,4096]{1,0:T(8,128)(2,1)S(1)}, u32[]{:S(2)}, u32[]{:S(2)}) %collective-permute-start.6) | collective-permute-done | bytes 196640 | tf_op jit(solution)/shard_map/ppermute | solution.py:23
  25.8 0.0 collective-permute-done.7
  25.9 2.9 %tables.2.refs_5_ = f32[1248,64]{1,0:T(8,128)S(1)} custom-call(bf16[24,4096]{1,0:T(8,128)(2,1)S(1)} %get-tuple-element.5.refs_0_, bf16[24,4096]{1,0:T(8,128)(2,1)S(1)} %get-tuple-element.10.refs_1_, bf16[24,4096]{1,0:T(8,128)(2,1)S(1)} %get-tuple-element.8.refs_2_, bf16[24,4096]{1,0:T(8,128)(2,1)S(1)} %get-tuple-element.9.refs_3_, ...), custom_call_target="tpu_custom_call" | custom-call | flops 2617245696 | bytes 983040 | tf_op jit(solution)/shard_map/tables/pallas_call | solution.py:96
  28.8 0.0 collective-permute-done.2
  28.8 0.0 collective-permute-done.3
  28.9 3.0 %tables.3 = f32[2,4,96,128]{3,2,1,0:T(8,128)S(1)} custom-call(bf16[24,4096]{1,0:T(8,128)(2,1)S(1)} %get-tuple-element.6.refs_0_, bf16[24,4096]{1,0:T(8,128)(2,1)S(1)} %get-tuple-element.14.refs_1_, bf16[24,4096]{1,0:T(8,128)(2,1)S(1)} %get-tuple-element.12.refs_2_, bf16[24,4096]{1,0:T(8,128)(2,1)S(1)} %get-tuple-element.13.refs_3_, ...), custom_call_target="tpu_custom_call" | custom-call | flops 2617245696 | bytes 983040 | tf_op jit(solution)/shard_map/tables/pallas_call | solution.py:96
  31.9 0.1 collective-permute-start.8
  32.0 1.4 %collective-permute-done.8 = f32[4,96,128]{2,1,0:T(8,128)S(1)} collective-permute-done((f32[4,96,128]{2,1,0:T(8,128)S(1)}, f32[4,96,128]{2,1,0:T(8,128)S(1)}, u32[]{:S(2)}, u32[]{:S(2)}) %collective-permute-start.8) | collective-permute-done | bytes 196640 | tf_op jit(solution)/shard_map/ppermute | solution.py:177
  33.5 0.6 %dynamic-slice_bitcast_fusion.1 = (f32[96,128]{1,0:T(8,128)S(1)}, f32[96,128]{1,0:T(8,128)S(1)}, f32[96,128]{1,0:T(8,128)S(1)}, f32[1,96,128]{2,1,0:T(8,128)}) fusion(f32[4,96,128]{2,1,0:T(8,128)S(1)} %bitcast_add_fusion, s32[]{:T(128)S(6)} %select_n.86, s32[]{:T(128)S(6)} %select_n.85, s32[]{:T(128)S(6)} %select_n.84, s32[]{:T(128)S(6)} %select_n.83), kind=kLoop, calls=%fused_computation.10 | loop fusion | bytes 393232 | tf_op jit(solution)/shard_map/jit(dynamic_index_in_dim)/squeeze | solution.py:180
  34.1 1.5 %collective-permute-start.10 = (f32[96,128]{1,0:T(8,128)S(1)}, f32[96,128]{1,0:T(8,128)S(1)}, u32[]{:S(2)}, u32[]{:S(2)}) collective-permute-start(f32[96,128]{1,0:T(8,128)S(1)} %get-tuple-element.16), channel_id=1, source_target_pairs={{0,5},{1,4},{4,1},{5,0},{2,7},{3,6},{6,3},{7,2},{8,13},{9,12},{12,... | collective-permute-start | bytes 147464 | tf_op jit(solution)/shard_map/ppermute | solution.py:27
  35.6 1.8 %collective-permute-start.11 = (f32[96,128]{1,0:T(8,128)S(1)}, f32[96,128]{1,0:T(8,128)S(1)}, u32[]{:S(2)}, u32[]{:S(2)}) collective-permute-start(f32[96,128]{1,0:T(8,128)S(1)} %get-tuple-element.15), channel_id=1, source_target_pairs={{0,4},{1,5},{4,0},{5,1},{2,6},{3,7},{6,2},{7,3},{8,12},{9,13},{12,... | collective-permute-start | bytes 147464 | tf_op jit(solution)/shard_map/ppermute | solution.py:27
  37.4 0.2 collective-permute-start.9
  37.6 0.6 %collective-permute-done.10.two_ref = f32[96,128]{1,0:T(8,128)S(1)} collective-permute-done((f32[96,128]{1,0:T(8,128)S(1)}, f32[96,128]{1,0:T(8,128)S(1)}, u32[]{:S(2)}, u32[]{:S(2)}) %collective-permute-start.10) | collective-permute-done | bytes 49184 | tf_op jit(solution)/shard_map/ppermute | solution.py:27
  38.2 0.0 copy-start
  38.2 1.7 %collective-permute-done.11.three_ref = f32[96,128]{1,0:T(8,128)S(1)} collective-permute-done((f32[96,128]{1,0:T(8,128)S(1)}, f32[96,128]{1,0:T(8,128)S(1)}, u32[]{:S(2)}, u32[]{:S(2)}) %collective-permute-start.11) | collective-permute-done | bytes 49184 | tf_op jit(solution)/shard_map/ppermute | solution.py:27
  39.9 0.0 copy-start.1
  39.9 3.1 %collective-permute-done.9.one_ref = f32[96,128]{1,0:T(8,128)S(1)} collective-permute-done((f32[96,128]{1,0:T(8,128)S(1)}, f32[96,128]{1,0:T(8,128)S(1)}, u32[]{:S(2)}, u32[]{:S(2)}) %collective-permute-start.9) | collective-permute-done | bytes 49184 | tf_op jit(solution)/shard_map/ppermute | solution.py:27
  43.0 0.0 copy-start.2
  43.0 0.0 copy-done
  43.0 0.0 copy-done.1
  43.0 0.6 %copy-done.2 = f32[96,128]{1,0:T(8,128)} copy-done((f32[96,128]{1,0:T(8,128)}, f32[96,128]{1,0:T(8,128)S(1)}, u32[]{:S(2)}) %copy-start.2) | copy-done | bytes 49176
  43.6 1.9 %finish.1 = f32[6,2,48,96]{3,2,1,0:T(8,128)} custom-call(f32[1,96,128]{2,1,0:T(8,128)} %get-tuple-element.18.own_ref, f32[96,128]{1,0:T(8,128)} %copy-done.2, f32[96,128]{1,0:T(8,128)} %copy-done, f32[96,128]{1,0:T(8,128)} %copy-done.1), custom_call_target="tpu_custom_call" | custom-call | tf_op jit(solution)/shard_map/finish/pallas_call | solution.py:151
  (6 shorter events, 0.2 us)
Async XLA Ops:
  1.1 11.4 %collective-permute-start.5 = (bf16[24,4096]{1,0:T(8,128)(2,1)S(1)}, bf16[24,4096]{1,0:T(8,128)(2,1)S(1)}, u32[]{:S(2)}, u32[]{:S(2)}) collective-permute-start(bf16[24,4096]{1,0:T(8,128)(2,1)S(1)} %get-tuple-element.5.refs_0_), channel_id=1, source_target_pairs={{0,8},{8,0},{16,24},{24,16},{32,40},{40,32},{48,56},{56,48},{64,72... | collective-permute-start | bytes 589832 | tf_op jit(solution)/shard_map/ppermute | solution.py:23
  3.1 14.2 %collective-permute-start.4 = (bf16[24,4096]{1,0:T(8,128)(2,1)S(1)}, bf16[24,4096]{1,0:T(8,128)(2,1)S(1)}, u32[]{:S(2)}, u32[]{:S(2)}) collective-permute-start(bf16[24,4096]{1,0:T(8,128)(2,1)S(1)} %get-tuple-element.5.refs_0_), channel_id=1, source_target_pairs={{0,248},{8,16},{16,8},{24,32},{32,24},{40,48},{48,40},{56,64},{64,... | collective-permute-start | bytes 589832 | tf_op jit(solution)/shard_map/ppermute | solution.py:23
  10.5 6.8 %collective-permute-start.1 = (bf16[24,4096]{1,0:T(8,128)(2,1)S(1)}, bf16[24,4096]{1,0:T(8,128)(2,1)S(1)}, u32[]{:S(2)}, u32[]{:S(2)}) collective-permute-start(bf16[24,4096]{1,0:T(8,128)(2,1)S(1)} %get-tuple-element.6.refs_0_), channel_id=1, source_target_pairs={{0,8},{8,0},{16,24},{24,16},{32,40},{40,32},{48,56},{56,48},{64,72... | collective-permute-start | bytes 589832 | tf_op jit(solution)/shard_map/ppermute | solution.py:23
  10.5 11.3 %collective-permute-start = (bf16[24,4096]{1,0:T(8,128)(2,1)S(1)}, bf16[24,4096]{1,0:T(8,128)(2,1)S(1)}, u32[]{:S(2)}, u32[]{:S(2)}) collective-permute-start(bf16[24,4096]{1,0:T(8,128)(2,1)S(1)} %get-tuple-element.6.refs_0_), channel_id=1, source_target_pairs={{0,248},{8,16},{16,8},{24,32},{32,24},{40,48},{48,40},{56,64},{64,... | collective-permute-start | bytes 589832 | tf_op jit(solution)/shard_map/ppermute | solution.py:23
  12.5 13.4 %collective-permute-start.6 = (bf16[24,4096]{1,0:T(8,128)(2,1)S(1)}, bf16[24,4096]{1,0:T(8,128)(2,1)S(1)}, u32[]{:S(2)}, u32[]{:S(2)}) collective-permute-start(bf16[24,4096]{1,0:T(8,128)(2,1)S(1)} %collective-permute-done.5), channel_id=1, source_target_pairs={{0,248},{8,16},{16,8},{24,32},{32,24},{40,48},{48,40},{56,64},{64,... | collective-permute-start | bytes 589832 | tf_op jit(solution)/shard_map/ppermute | solution.py:23
  17.2 8.6 %collective-permute-start.7 = (bf16[24,4096]{1,0:T(8,128)(2,1)S(1)}, bf16[24,4096]{1,0:T(8,128)(2,1)S(1)}, u32[]{:S(2)}, u32[]{:S(2)}) collective-permute-start(bf16[24,4096]{1,0:T(8,128)(2,1)S(1)} %collective-permute-done.4), channel_id=1, source_target_pairs={{0,8},{8,0},{16,24},{24,16},{32,40},{40,32},{48,56},{56,48},{64,72... | collective-permute-start | bytes 589832 | tf_op jit(solution)/shard_map/ppermute | solution.py:23
  17.3 11.5 %collective-permute-start.2 = (bf16[24,4096]{1,0:T(8,128)(2,1)S(1)}, bf16[24,4096]{1,0:T(8,128)(2,1)S(1)}, u32[]{:S(2)}, u32[]{:S(2)}) collective-permute-start(bf16[24,4096]{1,0:T(8,128)(2,1)S(1)} %collective-permute-done.1), channel_id=1, source_target_pairs={{0,248},{8,16},{16,8},{24,32},{32,24},{40,48},{48,40},{56,64},{64,... | collective-permute-start | bytes 589832 | tf_op jit(solution)/shard_map/ppermute | solution.py:23
  21.7 7.1 %collective-permute-start.3 = (bf16[24,4096]{1,0:T(8,128)(2,1)S(1)}, bf16[24,4096]{1,0:T(8,128)(2,1)S(1)}, u32[]{:S(2)}, u32[]{:S(2)}) collective-permute-start(bf16[24,4096]{1,0:T(8,128)(2,1)S(1)} %collective-permute-done), channel_id=1, source_target_pairs={{0,8},{8,0},{16,24},{24,16},{32,40},{40,32},{48,56},{56,48},{64,72... | collective-permute-start | bytes 589832 | tf_op jit(solution)/shard_map/ppermute | solution.py:23
  31.9 1.5 %collective-permute-start.8 = (f32[4,96,128]{2,1,0:T(8,128)S(1)}, f32[4,96,128]{2,1,0:T(8,128)S(1)}, u32[]{:S(2)}, u32[]{:S(2)}) collective-permute-start(f32[4,96,128]{2,1,0:T(8,128)S(1)} %dynamic-slice_bitcast_fusion), channel_id=1, source_target_pairs={{0,2},{2,0},{1,3},{3,1},{4,6},{6,4},{5,7},{7,5},{8,10},{10,8},{9,1... | collective-permute-start | bytes 589832 | tf_op jit(solution)/shard_map/ppermute | solution.py:177
  34.1 4.1 %collective-permute-start.10 = (f32[96,128]{1,0:T(8,128)S(1)}, f32[96,128]{1,0:T(8,128)S(1)}, u32[]{:S(2)}, u32[]{:S(2)}) collective-permute-start(f32[96,128]{1,0:T(8,128)S(1)} %get-tuple-element.16), channel_id=1, source_target_pairs={{0,5},{1,4},{4,1},{5,0},{2,7},{3,6},{6,3},{7,2},{8,13},{9,12},{12,... | collective-permute-start | bytes 147464 | tf_op jit(solution)/shard_map/ppermute | solution.py:27
  35.6 4.3 %collective-permute-start.11 = (f32[96,128]{1,0:T(8,128)S(1)}, f32[96,128]{1,0:T(8,128)S(1)}, u32[]{:S(2)}, u32[]{:S(2)}) collective-permute-start(f32[96,128]{1,0:T(8,128)S(1)} %get-tuple-element.15), channel_id=1, source_target_pairs={{0,4},{1,5},{4,0},{5,1},{2,6},{3,7},{6,2},{7,3},{8,12},{9,13},{12,... | collective-permute-start | bytes 147464 | tf_op jit(solution)/shard_map/ppermute | solution.py:27
  37.4 5.6 %collective-permute-start.9 = (f32[96,128]{1,0:T(8,128)S(1)}, f32[96,128]{1,0:T(8,128)S(1)}, u32[]{:S(2)}, u32[]{:S(2)}) collective-permute-start(f32[96,128]{1,0:T(8,128)S(1)} %get-tuple-element.17), channel_id=1, source_target_pairs={{0,1},{1,0},{4,5},{5,4},{2,3},{3,2},{6,7},{7,6},{8,9},{9,8},{12,13... | collective-permute-start | bytes 147464 | tf_op jit(solution)/shard_map/ppermute | solution.py:27
  38.2 4.8 %copy-start = (f32[96,128]{1,0:T(8,128)}, f32[96,128]{1,0:T(8,128)S(1)}, u32[]{:S(2)}) copy-start(f32[96,128]{1,0:T(8,128)S(1)} %collective-permute-done.10.two_ref) | copy-start | bytes 147460
  39.9 3.1 %copy-start.1 = (f32[96,128]{1,0:T(8,128)}, f32[96,128]{1,0:T(8,128)S(1)}, u32[]{:S(2)}) copy-start(f32[96,128]{1,0:T(8,128)S(1)} %collective-permute-done.11.three_ref) | copy-start | bytes 147460
  43.0 0.6 %copy-start.2 = (f32[96,128]{1,0:T(8,128)}, f32[96,128]{1,0:T(8,128)S(1)}, u32[]{:S(2)}) copy-start(f32[96,128]{1,0:T(8,128)S(1)} %collective-permute-done.9.one_ref) | copy-start | bytes 147460

commit v3 on v2

--- a/solution.py
+++ b/solution.py
@@ -151,6 +151,7 @@
     return pl.pallas_call(
         finish_kernel,
         out_shape=jax.ShapeDtypeStruct((SHARE, 2, 2 * VB, 96), jnp.float32),
+        compiler_params=pltpu.CompilerParams(vmem_limit_bytes=8 * 2**20),
         name="finish",
     )(*parts)
 
@@ -164,6 +165,7 @@
     own, at = [], 0
     for width in WIDTHS:
         own.append(lax.dynamic_slice_in_dim(dosage, rep * half + at, width, 1))
+        dosage, own[-1] = lax.optimization_barrier((dosage, own[-1]))
         at += width
     near = [(swapped(u, 0), swapped(u, 1)) for u in own]
     far = [(swapped(o, 0), swapped(e, 1)) for e, o in near]
@@ -176,7 +178,7 @@
     sent = lax.dynamic_index_in_dim(state, 1 - core, 0, False)
     kept = kept + lax.ppermute(sent, "core", SWAP)
     parts = [lax.dynamic_slice_in_dim(kept, chip, 1, 0)]
-    for flip in (1, 3, 2):
+    for flip in (2, 3, 1):
         parts.append(to_chip(lax.dynamic_index_in_dim(kept, chip ^ flip, 0, False), flip))
     return finish(parts).reshape(1, SHARE, 2, VB, 2, 96)
 

time: 45.6 us -> 43 us (0.943)
  the two profiles are of different devices: /device:TPU:2 before, /device:TPU:1 now
where the time goes in v3:
time: 43 us; the launch traced here: 42.9 us
  starting transfers between devices  24.8 us (58%)
  waiting for transfers between devices  9.77 us (23%)
  Pallas kernels  6.93 us (16%)
  local copies, waits for them, and re-layouts  1.2 us (3%)
    ppermute x8, starting transfers between devices, swapped(): return lax.ppermute(value, 'vec', pairs)  18.7 us
    pallas_call x2, Pallas kernels, tables_of(): pl.pallas_call(kernel, out_shape=jax.ShapeDtypeStruct(shape, jnp.float32)...  5.94 us
    ppermute x8, waiting for transfers between devices, swapped(): return lax.ppermute(value, 'vec', pairs)  5.02 us
    ppermute x3, waiting for transfers between devices, to_chip(): lax.ppermute(value, ('xlo', 'rep'), [(i, i ^ flip) for i in range(4)])  3.67 us
    ppermute x3, starting transfers between devices, to_chip(): lax.ppermute(value, ('xlo', 'rep'), [(i, i ^ flip) for i in range(4)])  3.34 us
    ppermute x1, starting transfers between devices, body(): kept = kept + lax.ppermute(sent, 'core', SWAP)  2.79 us
    unnamed x2, local copies, waits for them, and re-layouts  1.13 us
    ppermute x1, waiting for transfers between devices, body(): kept = kept + lax.ppermute(sent, 'core', SWAP)  1.07 us
  transfers between devices with their start and end apart: 12, of which 6 were waited for; matrix products, arithmetic and copies ran while one was open for 0% of the time, Pallas kernels for 7%

profile of v3, /device:TPU:1, one launch (start us, length us, event | category | flops | bytes accessed | tf_op | source)
XLA Modules:
  0.0 42.9 jit_solution(887095535091878337)
XLA Ops:
  0.0 0.0 copy-start
  0.0 1.1 %copy-done = bf16[24,16384]{1,0:T(8,128)(2,1)S(1)} copy-done((bf16[24,16384]{1,0:T(8,128)(2,1)S(1)}, bf16[24,16384]{1,0:T(8,128)(2,1)}, u32[]{:S(2)}) %copy-start) | copy-done | bytes 786456
  1.2 2.6 %collective-permute-start.5 = (bf16[24,4096]{1,0:T(8,128)(2,1)S(1)}, bf16[24,4096]{1,0:T(8,128)(2,1)S(1)}, u32[]{:S(2)}, u32[]{:S(2)}) collective-permute-start(bf16[24,4096]{1,0:T(8,128)(2,1)S(1)} %constant_dynamic-slice_fusion.2.refs_0_), channel_id=1, source_target_pairs={{0,8},{8,0},{16,24},{24,16},{32,40},{40,32},{48,56},{56,48},{64,72... | collective-permute-start | bytes 589832 | tf_op jit(solution)/shard_map/ppermute | solution.py:23
  3.7 7.1 %collective-permute-start.4 = (bf16[24,4096]{1,0:T(8,128)(2,1)S(1)}, bf16[24,4096]{1,0:T(8,128)(2,1)S(1)}, u32[]{:S(2)}, u32[]{:S(2)}) collective-permute-start(bf16[24,4096]{1,0:T(8,128)(2,1)S(1)} %constant_dynamic-slice_fusion.2.refs_0_), channel_id=1, source_target_pairs={{0,248},{8,16},{16,8},{24,32},{32,24},{40,48},{48,40},{56,64},{64,... | collective-permute-start | bytes 589832 | tf_op jit(solution)/shard_map/ppermute | solution.py:23
  10.8 0.1 collective-permute-start.1
  10.9 1.4 %collective-permute-start = (bf16[24,4096]{1,0:T(8,128)(2,1)S(1)}, bf16[24,4096]{1,0:T(8,128)(2,1)S(1)}, u32[]{:S(2)}, u32[]{:S(2)}) collective-permute-start(bf16[24,4096]{1,0:T(8,128)(2,1)S(1)} %constant_dynamic-slice_fusion.1.refs_0_), channel_id=1, source_target_pairs={{0,248},{8,16},{16,8},{24,32},{32,24},{40,48},{48,40},{56,64},{64,... | collective-permute-start | bytes 589832 | tf_op jit(solution)/shard_map/ppermute | solution.py:23
  12.4 0.0 collective-permute-done.5
  12.4 3.5 %collective-permute-start.6 = (bf16[24,4096]{1,0:T(8,128)(2,1)S(1)}, bf16[24,4096]{1,0:T(8,128)(2,1)S(1)}, u32[]{:S(2)}, u32[]{:S(2)}) collective-permute-start(bf16[24,4096]{1,0:T(8,128)(2,1)S(1)} %collective-permute-done.5), channel_id=1, source_target_pairs={{0,248},{8,16},{16,8},{24,32},{32,24},{40,48},{48,40},{56,64},{64,... | collective-permute-start | bytes 589832 | tf_op jit(solution)/shard_map/ppermute | solution.py:23
  15.9 0.0 collective-permute-done.4
  15.9 0.0 collective-permute-start.7
  15.9 0.2 collective-permute-done.1
  16.1 4.0 %collective-permute-start.2 = (bf16[24,4096]{1,0:T(8,128)(2,1)S(1)}, bf16[24,4096]{1,0:T(8,128)(2,1)S(1)}, u32[]{:S(2)}, u32[]{:S(2)}) collective-permute-start(bf16[24,4096]{1,0:T(8,128)(2,1)S(1)} %collective-permute-done.1), channel_id=1, source_target_pairs={{0,248},{8,16},{16,8},{24,32},{32,24},{40,48},{48,40},{56,64},{64,... | collective-permute-start | bytes 589832 | tf_op jit(solution)/shard_map/ppermute | solution.py:23
  20.1 0.0 collective-permute-done
  20.1 0.0 collective-permute-start.3
  20.1 3.6 %collective-permute-done.6 = bf16[24,4096]{1,0:T(8,128)(2,1)S(1)} collective-permute-done((bf16[24,4096]{1,0:T(8,128)(2,1)S(1)}, bf16[24,4096]{1,0:T(8,128)(2,1)S(1)}, u32[]{:S(2)}, u32[]{:S(2)}) %collective-permute-start.6) | collective-permute-done | bytes 196640 | tf_op jit(solution)/shard_map/ppermute | solution.py:23
  23.7 0.0 collective-permute-done.7
  23.8 2.9 %tables.2.refs_5_ = f32[1248,64]{1,0:T(8,128)S(1)} custom-call(bf16[24,4096]{1,0:T(8,128)(2,1)S(1)} %constant_dynamic-slice_fusion.2.refs_0_, bf16[24,4096]{1,0:T(8,128)(2,1)S(1)} %get-tuple-element.14.refs_1_, bf16[24,4096]{1,0:T(8,128)(2,1)S(1)} %get-tuple-element.12.refs_2_, bf16[24,4096]{1,0:T(8,128)(2,1)S(1)} %get-tuple-element.13.refs_3_, ...), custom_call_target="tpu_custom_call" | custom-call | flops 2617245696 | bytes 983040 | tf_op jit(solution)/shard_map/tables/pallas_call | solution.py:96
  26.7 1.2 %collective-permute-done.2 = bf16[24,4096]{1,0:T(8,128)(2,1)S(1)} collective-permute-done((bf16[24,4096]{1,0:T(8,128)(2,1)S(1)}, bf16[24,4096]{1,0:T(8,128)(2,1)S(1)}, u32[]{:S(2)}, u32[]{:S(2)}) %collective-permute-start.2) | collective-permute-done | bytes 196640 | tf_op jit(solution)/shard_map/ppermute | solution.py:23
  27.9 0.0 collective-permute-done.3
  28.0 3.0 %tables.3 = f32[2,4,96,128]{3,2,1,0:T(8,128)S(1)} custom-call(bf16[24,4096]{1,0:T(8,128)(2,1)S(1)} %constant_dynamic-slice_fusion.1.refs_0_, bf16[24,4096]{1,0:T(8,128)(2,1)S(1)} %get-tuple-element.18.refs_1_, bf16[24,4096]{1,0:T(8,128)(2,1)S(1)} %get-tuple-element.16.refs_2_, bf16[24,4096]{1,0:T(8,128)(2,1)S(1)} %get-tuple-element.17.refs_3_, ...), custom_call_target="tpu_custom_call" | custom-call | flops 2617245696 | bytes 983040 | tf_op jit(solution)/shard_map/tables/pallas_call | solution.py:96
  31.0 2.8 %collective-permute-start.8 = (f32[4,96,128]{2,1,0:T(8,128)S(1)}, f32[4,96,128]{2,1,0:T(8,128)S(1)}, u32[]{:S(2)}, u32[]{:S(2)}) collective-permute-start(f32[4,96,128]{2,1,0:T(8,128)S(1)} %dynamic-slice_bitcast_fusion), channel_id=1, source_target_pairs={{0,2},{2,0},{1,3},{3,1},{4,6},{6,4},{5,7},{7,5},{8,10},{10,8},{9,1... | collective-permute-start | bytes 589832 | tf_op jit(solution)/shard_map/ppermute | solution.py:179
  33.8 1.1 %collective-permute-done.8 = f32[4,96,128]{2,1,0:T(8,128)S(1)} collective-permute-done((f32[4,96,128]{2,1,0:T(8,128)S(1)}, f32[4,96,128]{2,1,0:T(8,128)S(1)}, u32[]{:S(2)}, u32[]{:S(2)}) %collective-permute-start.8) | collective-permute-done | bytes 196640 | tf_op jit(solution)/shard_map/ppermute | solution.py:179
  34.9 2.6 %collective-permute-start.10 = (f32[96,128]{1,0:T(8,128)S(1)}, f32[96,128]{1,0:T(8,128)S(1)}, u32[]{:S(2)}, u32[]{:S(2)}) collective-permute-start(f32[96,128]{1,0:T(8,128)S(1)} %get-tuple-element.20), channel_id=1, source_target_pairs={{0,5},{1,4},{4,1},{5,0},{2,7},{3,6},{6,3},{7,2},{8,13},{9,12},{12,... | collective-permute-start | bytes 147464 | tf_op jit(solution)/shard_map/ppermute | solution.py:27
  37.5 0.5 %collective-permute-start.11 = (f32[96,128]{1,0:T(8,128)S(1)}, f32[96,128]{1,0:T(8,128)S(1)}, u32[]{:S(2)}, u32[]{:S(2)}) collective-permute-start(f32[96,128]{1,0:T(8,128)S(1)} %get-tuple-element.19), channel_id=1, source_target_pairs={{0,1},{1,0},{4,5},{5,4},{2,3},{3,2},{6,7},{7,6},{8,9},{9,8},{12,13... | collective-permute-start | bytes 147464 | tf_op jit(solution)/shard_map/ppermute | solution.py:27
  38.0 0.3 collective-permute-start.9
  38.3 0.9 %collective-permute-done.10.two_ref = f32[96,128]{1,0:T(8,128)S(1)} collective-permute-done((f32[96,128]{1,0:T(8,128)S(1)}, f32[96,128]{1,0:T(8,128)S(1)}, u32[]{:S(2)}, u32[]{:S(2)}) %collective-permute-start.10) | collective-permute-done | bytes 49184 | tf_op jit(solution)/shard_map/ppermute | solution.py:27
  39.2 2.8 %collective-permute-done.11.three_ref = f32[96,128]{1,0:T(8,128)S(1)} collective-permute-done((f32[96,128]{1,0:T(8,128)S(1)}, f32[96,128]{1,0:T(8,128)S(1)}, u32[]{:S(2)}, u32[]{:S(2)}) %collective-permute-start.11) | collective-permute-done | bytes 49184 | tf_op jit(solution)/shard_map/ppermute | solution.py:27
  41.9 0.0 collective-permute-done.9.one_ref
  41.9 1.0 %finish.1 = f32[6,2,48,96]{3,2,1,0:T(8,128)} custom-call(f32[1,96,128]{2,1,0:T(8,128)S(1)} %get-tuple-element.22.own_ref, f32[96,128]{1,0:T(8,128)S(1)} %collective-permute-done.9.one_ref, f32[96,128]{1,0:T(8,128)S(1)} %collective-permute-done.10.two_ref, f32[96,128]{1,0:T(8,128)S(1)} %collective-permute-done.11.three_ref), custom_call_target="tpu_custom_call" | custom-call | tf_op jit(solution)/shard_map/finish/pallas_call | solution.py:151
  (9 shorter events, 0.2 us)
Async XLA Ops:
  0.0 1.1 %copy-start = (bf16[24,16384]{1,0:T(8,128)(2,1)S(1)}, bf16[24,16384]{1,0:T(8,128)(2,1)}, u32[]{:S(2)}) copy-start(bf16[24,16384]{1,0:T(8,128)(2,1)} %param.1) | copy-start | bytes 2359300
  1.2 11.2 %collective-permute-start.5 = (bf16[24,4096]{1,0:T(8,128)(2,1)S(1)}, bf16[24,4096]{1,0:T(8,128)(2,1)S(1)}, u32[]{:S(2)}, u32[]{:S(2)}) collective-permute-start(bf16[24,4096]{1,0:T(8,128)(2,1)S(1)} %constant_dynamic-slice_fusion.2.refs_0_), channel_id=1, source_target_pairs={{0,8},{8,0},{16,24},{24,16},{32,40},{40,32},{48,56},{56,48},{64,72... | collective-permute-start | bytes 589832 | tf_op jit(solution)/shard_map/ppermute | solution.py:23
  3.7 12.2 %collective-permute-start.4 = (bf16[24,4096]{1,0:T(8,128)(2,1)S(1)}, bf16[24,4096]{1,0:T(8,128)(2,1)S(1)}, u32[]{:S(2)}, u32[]{:S(2)}) collective-permute-start(bf16[24,4096]{1,0:T(8,128)(2,1)S(1)} %constant_dynamic-slice_fusion.2.refs_0_), channel_id=1, source_target_pairs={{0,248},{8,16},{16,8},{24,32},{32,24},{40,48},{48,40},{56,64},{64,... | collective-permute-start | bytes 589832 | tf_op jit(solution)/shard_map/ppermute | solution.py:23
  10.8 5.2 %collective-permute-start.1 = (bf16[24,4096]{1,0:T(8,128)(2,1)S(1)}, bf16[24,4096]{1,0:T(8,128)(2,1)S(1)}, u32[]{:S(2)}, u32[]{:S(2)}) collective-permute-start(bf16[24,4096]{1,0:T(8,128)(2,1)S(1)} %constant_dynamic-slice_fusion.1.refs_0_), channel_id=1, source_target_pairs={{0,8},{8,0},{16,24},{24,16},{32,40},{40,32},{48,56},{56,48},{64,72... | collective-permute-start | bytes 589832 | tf_op jit(solution)/shard_map/ppermute | solution.py:23
  10.9 9.1 %collective-permute-start = (bf16[24,4096]{1,0:T(8,128)(2,1)S(1)}, bf16[24,4096]{1,0:T(8,128)(2,1)S(1)}, u32[]{:S(2)}, u32[]{:S(2)}) collective-permute-start(bf16[24,4096]{1,0:T(8,128)(2,1)S(1)} %constant_dynamic-slice_fusion.1.refs_0_), channel_id=1, source_target_pairs={{0,248},{8,16},{16,8},{24,32},{32,24},{40,48},{48,40},{56,64},{64,... | collective-permute-start | bytes 589832 | tf_op jit(solution)/shard_map/ppermute | solution.py:23
  12.4 11.3 %collective-permute-start.6 = (bf16[24,4096]{1,0:T(8,128)(2,1)S(1)}, bf16[24,4096]{1,0:T(8,128)(2,1)S(1)}, u32[]{:S(2)}, u32[]{:S(2)}) collective-permute-start(bf16[24,4096]{1,0:T(8,128)(2,1)S(1)} %collective-permute-done.5), channel_id=1, source_target_pairs={{0,248},{8,16},{16,8},{24,32},{32,24},{40,48},{48,40},{56,64},{64,... | collective-permute-start | bytes 589832 | tf_op jit(solution)/shard_map/ppermute | solution.py:23
  15.9 7.9 %collective-permute-start.7 = (bf16[24,4096]{1,0:T(8,128)(2,1)S(1)}, bf16[24,4096]{1,0:T(8,128)(2,1)S(1)}, u32[]{:S(2)}, u32[]{:S(2)}) collective-permute-start(bf16[24,4096]{1,0:T(8,128)(2,1)S(1)} %collective-permute-done.4), channel_id=1, source_target_pairs={{0,8},{8,0},{16,24},{24,16},{32,40},{40,32},{48,56},{56,48},{64,72... | collective-permute-start | bytes 589832 | tf_op jit(solution)/shard_map/ppermute | solution.py:23
  16.1 11.8 %collective-permute-start.2 = (bf16[24,4096]{1,0:T(8,128)(2,1)S(1)}, bf16[24,4096]{1,0:T(8,128)(2,1)S(1)}, u32[]{:S(2)}, u32[]{:S(2)}) collective-permute-start(bf16[24,4096]{1,0:T(8,128)(2,1)S(1)} %collective-permute-done.1), channel_id=1, source_target_pairs={{0,248},{8,16},{16,8},{24,32},{32,24},{40,48},{48,40},{56,64},{64,... | collective-permute-start | bytes 589832 | tf_op jit(solution)/shard_map/ppermute | solution.py:23
  20.1 7.9 %collective-permute-start.3 = (bf16[24,4096]{1,0:T(8,128)(2,1)S(1)}, bf16[24,4096]{1,0:T(8,128)(2,1)S(1)}, u32[]{:S(2)}, u32[]{:S(2)}) collective-permute-start(bf16[24,4096]{1,0:T(8,128)(2,1)S(1)} %collective-permute-done), channel_id=1, source_target_pairs={{0,8},{8,0},{16,24},{24,16},{32,40},{40,32},{48,56},{56,48},{64,72... | collective-permute-start | bytes 589832 | tf_op jit(solution)/shard_map/ppermute | solution.py:23
  31.0 3.9 %collective-permute-start.8 = (f32[4,96,128]{2,1,0:T(8,128)S(1)}, f32[4,96,128]{2,1,0:T(8,128)S(1)}, u32[]{:S(2)}, u32[]{:S(2)}) collective-permute-start(f32[4,96,128]{2,1,0:T(8,128)S(1)} %dynamic-slice_bitcast_fusion), channel_id=1, source_target_pairs={{0,2},{2,0},{1,3},{3,1},{4,6},{6,4},{5,7},{7,5},{8,10},{10,8},{9,1... | collective-permute-start | bytes 589832 | tf_op jit(solution)/shard_map/ppermute | solution.py:179
  34.9 4.2 %collective-permute-start.10 = (f32[96,128]{1,0:T(8,128)S(1)}, f32[96,128]{1,0:T(8,128)S(1)}, u32[]{:S(2)}, u32[]{:S(2)}) collective-permute-start(f32[96,128]{1,0:T(8,128)S(1)} %get-tuple-element.20), channel_id=1, source_target_pairs={{0,5},{1,4},{4,1},{5,0},{2,7},{3,6},{6,3},{7,2},{8,13},{9,12},{12,... | collective-permute-start | bytes 147464 | tf_op jit(solution)/shard_map/ppermute | solution.py:27
  37.5 4.4 %collective-permute-start.11 = (f32[96,128]{1,0:T(8,128)S(1)}, f32[96,128]{1,0:T(8,128)S(1)}, u32[]{:S(2)}, u32[]{:S(2)}) collective-permute-start(f32[96,128]{1,0:T(8,128)S(1)} %get-tuple-element.19), channel_id=1, source_target_pairs={{0,1},{1,0},{4,5},{5,4},{2,3},{3,2},{6,7},{7,6},{8,9},{9,8},{12,13... | collective-permute-start | bytes 147464 | tf_op jit(solution)/shard_map/ppermute | solution.py:27
  38.0 3.9 %collective-permute-start.9 = (f32[96,128]{1,0:T(8,128)S(1)}, f32[96,128]{1,0:T(8,128)S(1)}, u32[]{:S(2)}, u32[]{:S(2)}) collective-permute-start(f32[96,128]{1,0:T(8,128)S(1)} %get-tuple-element.21), channel_id=1, source_target_pairs={{0,4},{1,5},{4,0},{5,1},{2,6},{3,7},{6,2},{7,3},{8,12},{9,13},{12,... | collective-permute-start | bytes 147464 | tf_op jit(solution)/shard_map/ppermute | solution.py:27

commit v4 on v3

v4 whole, which is shorter than its diff:
```python
import jax
import jax.numpy as jnp
from jax import lax
from jax.experimental import pallas as pl
from jax.experimental.pallas import tpu as pltpu
from jax.sharding import Mesh, PartitionSpec as P

F = 65536
VB = 24
N_VEC = 32
SHARE = 6
E_WIDTHS = (4096, 4096)
O_WIDTHS = (4096, 4096)
SPANS = (4096, 4096)
STEP = 256
STREAMED = 9
CUT = STREAMED * 48 + 48
HELD = (VB - STREAMED) * 48 + 32
OWN = CUT + (VB - STREAMED) * 48
ROWS = CUT + HELD
COLS = 64
PACKED = 96
SWAP = ((0, 1), (1, 0))


def swapped(value, odd):
    pairs = [(i, (((i + odd) ^ 1) - odd) % N_VEC) for i in range(N_VEC)]
    return lax.ppermute(value, "vec", pairs)


def to_chip(value, flip):
    return lax.ppermute(value, ("xlo", "rep"), [(i, i ^ flip) for i in range(4)])


def taken(pieces, at, step):
    for start, ref in pieces:
        if start <= at < start + ref.shape[1]:
            return ref[:, at - start : at - start + step]


def accumulate(streams, span, acc_ref, held_ref, before):
    even = lax.axis_index("vec") % 2 == 0
    for at in range(*span, STEP):
        own, e, o, oe, eo = (taken(pieces, at, STEP) for pieces in streams)
        third = jnp.concatenate([jnp.where(even, o, e), jnp.where(even, oe, eo)], axis=0)
        ones = jnp.ones((16, STEP), jnp.bfloat16)
        partner = jnp.concatenate(
            [jnp.where(even, e, o), jnp.where(even, eo, oe), ones], axis=0
        )
        pairs = [own[i : i + 1, :] * third for i in range(VB)]
        streamed = jnp.concatenate(pairs[:STREAMED] + [third], axis=0)
        held = jnp.concatenate(pairs[STREAMED:] + [own, ones[:8]], axis=0)
        first = lax.dot_general(
            streamed, partner, (((1,), (1,)), ((), ())), preferred_element_type=jnp.float32
        )
        second = lax.dot_general(
            partner, held, (((1,), (1,)), ((), ())), preferred_element_type=jnp.float32
        )
        if at > span[0]:
            acc_ref[:CUT, :] += first
            held_ref[...] += second
        elif before is None:
            acc_ref[:CUT, :] = first
            held_ref[...] = second
        else:
            acc_ref[:CUT, :] = before[0][:CUT, :] + first
            held_ref[...] = before[1][...] + second


def row_of(i):
    return i * 48 if i < STREAMED else CUT + (i - STREAMED) * 48


def pack(acc_ref, out_ref):
    for core in range(2):
        for chip in range(4):
            xlo, rep = divmod(chip, 2)
            q = xlo * 2 + core
            for ii in range(3):
                for half in range(2):
                    row = row_of(SHARE * q + 3 * half + ii) + VB * rep
                    out_ref[core, chip, ii * VB : (ii + 1) * VB, half * COLS : (half + 1) * COLS] = (
                        acc_ref[row : row + VB, :]
                    )
            out_ref[core, chip, 72:96, :COLS] = acc_ref[STREAMED * 48 + VB * rep : STREAMED * 48 + VB * (rep + 1), :]
            out_ref[core, chip, 72:80, COLS:] = jnp.concatenate(
                [
                    acc_ref[OWN + VB : OWN + VB + 1, :],
                    acc_ref[OWN + SHARE * q : OWN + SHARE * (q + 1), :],
                    jnp.zeros((1, COLS), jnp.float32),
                ],
                axis=0,
            )
            out_ref[core, chip, 80:96, COLS:] = jnp.zeros((16, COLS), jnp.float32)


def tables_of(streams, span, before, last):
    picked = [
        [(start, piece) for start, piece in stream if start < span[1] and start + piece.shape[1] > span[0]]
        for stream in streams
    ]
    order = (0, 1, 2, 3, 4)
    blocks = [piece for k in order for _, piece in picked[k]]

    def kernel(*refs):
        refs = list(refs)
        found = [None] * len(picked)
        for k in order:
            found[k] = [(start, refs.pop(0)) for start, _ in picked[k]]
        before_refs = None if before is None else (refs.pop(0), refs.pop(0))
        if last:
            out_ref, acc_ref, held_ref = refs
        else:
            acc_ref, held_ref = refs
        accumulate(found, span, acc_ref, held_ref, before_refs)
        if last:
            acc_ref[CUT:, :] = held_ref[...].T
            pack(acc_ref, out_ref)

    sums = [(CUT if not last else ROWS, COLS), (COLS, HELD)]
    packed = jax.ShapeDtypeStruct((2, 4, PACKED, 128), jnp.float32)
    width = span[1] - span[0]
    return pl.pallas_call(
        kernel,
        out_shape=packed if last else [jax.ShapeDtypeStruct(shape, jnp.float32) for shape in sums],
        scratch_shapes=[pltpu.VMEM(shape, jnp.float32) for shape in sums] if last else [],
        compiler_params=pltpu.CompilerParams(vmem_limit_bytes=32 * 2**20),
        cost_estimate=pl.CostEstimate(
            flops=2 * ROWS * width * 256, bytes_accessed=5 * VB * width * 2, transcendentals=0
        ),
        name="tables",
    )(*blocks, *(() if before is None else before))


def finish_kernel(own_ref, one_ref, two_ref, three_ref, out_ref):
    summed = (own_ref[0] + one_ref[...]) + (two_ref[...] + three_ref[...])
    row = lax.broadcasted_iota(jnp.int32, (128, 256), 0)
    col = lax.broadcasted_iota(jnp.int32, (128, 256), 1)
    same_half = (row >= COLS) == (col >= 128)
    lane = jnp.where(row >= COLS, row - COLS, row)
    target = jnp.where(col >= 128, col - 128, col)
    even = (target % 2) == 0
    inside = same_half & (target < 96)
    entry = jnp.where(inside & (target // 2 == lane), jnp.where(even, -1.0, 1.0), 0.0)
    entry = entry + jnp.where(inside & even & (lane == 48), 2.0, 0.0)
    spread = jnp.dot(
        summed, entry, precision=lax.Precision.HIGHEST, preferred_element_type=jnp.float32
    )
    third_row = spread[72:96, :96]
    singles = spread[72:80, 128:224]
    ones_row = singles[0:1]

    def gain(total):
        return 1.0 - total / (3.0 * F)

    gain_partner = gain(ones_row) * (4.5 / (8.0 * F))
    third_total = summed[72:96, 48:49]
    own_total = summed[72:80, 112:113]
    third_gain = (gain(2.0 * F - third_total), gain(third_total))
    own_gain = (gain(2.0 * F - own_total), gain(own_total))
    for i in range(SHARE):
        half, ii = divmod(i, 3)
        pair = spread[ii * VB : (ii + 1) * VB, half * 128 : half * 128 + 96]
        own_row = singles[1 + i : 2 + i]
        by_place = {
            (1, 1): pair,
            (1, 0): 2.0 * own_row - pair,
            (0, 1): 2.0 * third_row - pair,
            (0, 0): (4.0 * ones_row - 2.0 * own_row) - (2.0 * third_row - pair),
        }
        for a in range(2):
            partner = gain_partner * own_gain[a][1 + i : 2 + i]
            for c in range(2):
                out_ref[i, a, pl.ds(c, VB, stride=2), :] = by_place[a, c] * third_gain[c] * partner


def finish(parts):
    return pl.pallas_call(
        finish_kernel,
        out_shape=jax.ShapeDtypeStruct((SHARE, 2, 2 * VB, 96), jnp.float32),
        compiler_params=pltpu.CompilerParams(vmem_limit_bytes=8 * 2**20),
        name="finish",
    )(*parts)


def body(dosage):
    rep = lax.axis_index("rep")
    core = lax.axis_index("core")
    chip = lax.axis_index("xlo") * 2 + rep
    half = dosage.shape[1] // 2

    def cut(dosage, at, width):
        piece = lax.dynamic_slice_in_dim(dosage, rep * half + at, width, 1)
        return lax.optimization_barrier((dosage, piece))

    def pieces(widths):
        at = 0
        for width in widths:
            yield at, width
            at += width

    own = []
    for at, width in pieces(E_WIDTHS):
        dosage, piece = cut(dosage, at, width)
        own.append((at, piece))
    e_own = o_own = own

    e = [(at, swapped(u, 0)) for at, u in e_own]
    o = [(at, swapped(u, 1)) for at, u in o_own]
    eo = [(at, swapped(v, 0)) for at, v in o]
    oe = [(at, swapped(v, 1)) for at, v in e]
    state = None
    for at, width in pieces(SPANS):
        span = (at, at + width)
        state = tables_of((e_own, e, o, oe, eo), span, state, span[1] == half)
    kept = lax.dynamic_index_in_dim(state, core, 0, False)
    sent = lax.dynamic_index_in_dim(state, 1 - core, 0, False)
    kept = kept + lax.ppermute(sent, "core", SWAP)
    parts = [lax.dynamic_slice_in_dim(kept, chip, 1, 0)]
    for flip in (2, 3, 1):
        parts.append(to_chip(lax.dynamic_index_in_dim(kept, chip ^ flip, 0, False), flip))
    return finish(parts).reshape(1, SHARE, 2, VB, 2, 96)


def solution(mesh):
    split = Mesh(mesh.devices.reshape(N_VEC, 2, 2, 2), ("vec", "xlo", "core", "rep"))
    return jax.shard_map(
        body,
        mesh=split,
        in_specs=(P("vec", ("xlo", "core")),),
        out_specs=P("rep", ("vec", "xlo", "core"), None, None, None, None),
        check_vma=False,
    )
```

time: 43 us -> 42.4 us (0.986)
  Pallas kernels: 6.93 us -> 6.36 us
  waiting for transfers between devices: 9.77 us -> 10.3 us
  starting transfers between devices: 24.8 us -> 24.3 us
    pallas_call x2, Pallas kernels: 5.94 us -> 5.37 us  [tables_of(): pl.pallas_call(kernel, out_shape=packed if last else [jax.ShapeDtypeStruc...]
    ppermute x8, waiting for transfers between devices: 5.02 us -> 5.57 us  [swapped(): return lax.ppermute(value, 'vec', pairs)]
    ppermute x1, starting transfers between devices: 2.79 us -> 2.31 us  [body(): kept = kept + lax.ppermute(sent, 'core', SWAP)]
  transfers between devices with their start and end apart: 12 -> 12, of which waited for: 6 -> 6; matrix products, arithmetic and copies ran while one was open for 0% -> 0% of each run, Pallas kernels for 7% -> 6%
where the time goes in v4:
time: 42.4 us; the launch traced here: 42.3 us
  starting transfers between devices  24.3 us (57%)
  waiting for transfers between devices  10.3 us (24%)
  Pallas kernels  6.36 us (15%)
  local copies, waits for them, and re-layouts  1.21 us (3%)
    ppermute x8, starting transfers between devices, swapped(): return lax.ppermute(value, 'vec', pairs)  18.7 us
    ppermute x8, waiting for transfers between devices, swapped(): return lax.ppermute(value, 'vec', pairs)  5.57 us
    pallas_call x2, Pallas kernels, tables_of(): pl.pallas_call(kernel, out_shape=packed if last else [jax.ShapeDtypeStruc...  5.37 us
    ppermute x3, waiting for transfers between devices, to_chip(): lax.ppermute(value, ('xlo', 'rep'), [(i, i ^ flip) for i in range(4)])  3.67 us
    ppermute x3, starting transfers between devices, to_chip(): lax.ppermute(value, ('xlo', 'rep'), [(i, i ^ flip) for i in range(4)])  3.34 us
    ppermute x1, starting transfers between devices, body(): kept = kept + lax.ppermute(sent, 'core', SWAP)  2.31 us
    unnamed x2, local copies, waits for them, and re-layouts  1.13 us
    ppermute x1, waiting for transfers between devices, body(): kept = kept + lax.ppermute(sent, 'core', SWAP)  1.07 us
  transfers between devices with their start and end apart: 12, of which 6 were waited for; matrix products, arithmetic and copies ran while one was open for 0% of the time, Pallas kernels for 6%

profile of v4, /device:TPU:1, one launch (start us, length us, event | category | flops | bytes accessed | tf_op | source)
XLA Modules:
  0.0 42.3 jit_solution(2305973911488434363)
XLA Ops:
  0.0 0.0 copy-start
  0.0 1.1 %copy-done = bf16[24,16384]{1,0:T(8,128)(2,1)S(1)} copy-done((bf16[24,16384]{1,0:T(8,128)(2,1)S(1)}, bf16[24,16384]{1,0:T(8,128)(2,1)}, u32[]{:S(2)}) %copy-start) | copy-done | bytes 786456
  1.2 2.6 %collective-permute-start.4 = (bf16[24,4096]{1,0:T(8,128)(2,1)S(1)}, bf16[24,4096]{1,0:T(8,128)(2,1)S(1)}, u32[]{:S(2)}, u32[]{:S(2)}) collective-permute-start(bf16[24,4096]{1,0:T(8,128)(2,1)S(1)} %constant_dynamic-slice_fusion.2.refs_0_), channel_id=1, source_target_pairs={{0,8},{8,0},{16,24},{24,16},{32,40},{40,32},{48,56},{56,48},{64,72... | collective-permute-start | bytes 589832 | tf_op jit(solution)/shard_map/ppermute | solution.py:28
  3.7 7.1 %collective-permute-start.5 = (bf16[24,4096]{1,0:T(8,128)(2,1)S(1)}, bf16[24,4096]{1,0:T(8,128)(2,1)S(1)}, u32[]{:S(2)}, u32[]{:S(2)}) collective-permute-start(bf16[24,4096]{1,0:T(8,128)(2,1)S(1)} %constant_dynamic-slice_fusion.2.refs_0_), channel_id=1, source_target_pairs={{0,248},{8,16},{16,8},{24,32},{32,24},{40,48},{48,40},{56,64},{64,... | collective-permute-start | bytes 589832 | tf_op jit(solution)/shard_map/ppermute | solution.py:28
  10.8 0.1 collective-permute-start
  10.9 1.4 %collective-permute-start.1 = (bf16[24,4096]{1,0:T(8,128)(2,1)S(1)}, bf16[24,4096]{1,0:T(8,128)(2,1)S(1)}, u32[]{:S(2)}, u32[]{:S(2)}) collective-permute-start(bf16[24,4096]{1,0:T(8,128)(2,1)S(1)} %constant_dynamic-slice_fusion.1.refs_0_), channel_id=1, source_target_pairs={{0,248},{8,16},{16,8},{24,32},{32,24},{40,48},{48,40},{56,64},{64,... | collective-permute-start | bytes 589832 | tf_op jit(solution)/shard_map/ppermute | solution.py:28
  12.4 0.0 collective-permute-done.4.refs_1_
  12.4 3.5 %collective-permute-start.6 = (bf16[24,4096]{1,0:T(8,128)(2,1)S(1)}, bf16[24,4096]{1,0:T(8,128)(2,1)S(1)}, u32[]{:S(2)}, u32[]{:S(2)}) collective-permute-start(bf16[24,4096]{1,0:T(8,128)(2,1)S(1)} %collective-permute-done.4.refs_1_), channel_id=1, source_target_pairs={{0,248},{8,16},{16,8},{24,32},{32,24},{40,48},{48,40},{56,64},{64,... | collective-permute-start | bytes 589832 | tf_op jit(solution)/shard_map/ppermute | solution.py:28
  15.9 0.0 collective-permute-done.5.refs_2_
  15.9 0.0 collective-permute-start.7
  15.9 0.2 collective-permute-done.refs_1_
  16.1 4.0 %collective-permute-start.2 = (bf16[24,4096]{1,0:T(8,128)(2,1)S(1)}, bf16[24,4096]{1,0:T(8,128)(2,1)S(1)}, u32[]{:S(2)}, u32[]{:S(2)}) collective-permute-start(bf16[24,4096]{1,0:T(8,128)(2,1)S(1)} %collective-permute-done.refs_1_), channel_id=1, source_target_pairs={{0,248},{8,16},{16,8},{24,32},{32,24},{40,48},{48,40},{56,64},{64,... | collective-permute-start | bytes 589832 | tf_op jit(solution)/shard_map/ppermute | solution.py:28
  20.1 0.0 collective-permute-done.1.refs_2_
  20.1 0.0 collective-permute-start.3
  20.1 3.6 %collective-permute-done.6.refs_3_ = bf16[24,4096]{1,0:T(8,128)(2,1)S(1)} collective-permute-done((bf16[24,4096]{1,0:T(8,128)(2,1)S(1)}, bf16[24,4096]{1,0:T(8,128)(2,1)S(1)}, u32[]{:S(2)}, u32[]{:S(2)}) %collective-permute-start.6) | collective-permute-done | bytes 196640 | tf_op jit(solution)/shard_map/ppermute | solution.py:28
  23.7 0.0 collective-permute-done.7.refs_4_
  23.7 2.5 %tables.2 = (f32[480,64]{1,0:T(8,128)S(1)}, f32[64,752]{1,0:T(8,128)S(1)}) custom-call(bf16[24,4096]{1,0:T(8,128)(2,1)S(1)} %constant_dynamic-slice_fusion.2.refs_0_, bf16[24,4096]{1,0:T(8,128)(2,1)S(1)} %collective-permute-done.4.refs_1_, bf16[24,4096]{1,0:T(8,128)(2,1)S(1)} %collective-permute-done.5.refs_2_, ...), custom_call_target="tpu_custom_call" | custom-call | flops 2583691264 | bytes 983040 | tf_op jit(solution)/shard_map/tables/pallas_call | solution.py:123
  26.2 1.7 %collective-permute-done.2.refs_3_ = bf16[24,4096]{1,0:T(8,128)(2,1)S(1)} collective-permute-done((bf16[24,4096]{1,0:T(8,128)(2,1)S(1)}, bf16[24,4096]{1,0:T(8,128)(2,1)S(1)}, u32[]{:S(2)}, u32[]{:S(2)}) %collective-permute-start.2) | collective-permute-done | bytes 196640 | tf_op jit(solution)/shard_map/ppermute | solution.py:28
  27.9 0.0 collective-permute-done.3.refs_4_
  27.9 2.9 %tables.3 = f32[2,4,96,128]{3,2,1,0:T(8,128)S(1)} custom-call(bf16[24,4096]{1,0:T(8,128)(2,1)S(1)} %constant_dynamic-slice_fusion.1.refs_0_, bf16[24,4096]{1,0:T(8,128)(2,1)S(1)} %collective-permute-done.refs_1_, bf16[24,4096]{1,0:T(8,128)(2,1)S(1)} %collective-permute-done.1.refs_2_, bf16[24,4096]{1,0:T(8,128)(2,1)S(1)} %collective-permute-done.2.refs_3_, ...), custom_call_target="tpu_custom_call" | custom-call | flops 2583691264 | bytes 983040 | tf_op jit(solution)/shard_map/tables/pallas_call | solution.py:123
  30.9 2.3 %collective-permute-start.8 = (f32[4,96,128]{2,1,0:T(8,128)S(1)}, f32[4,96,128]{2,1,0:T(8,128)S(1)}, u32[]{:S(2)}, u32[]{:S(2)}) collective-permute-start(f32[4,96,128]{2,1,0:T(8,128)S(1)} %dynamic-slice_bitcast_fusion), channel_id=1, source_target_pairs={{0,2},{2,0},{1,3},{3,1},{4,6},{6,4},{5,7},{7,5},{8,10},{10,8},{9,1... | collective-permute-start | bytes 589832 | tf_op jit(solution)/shard_map/ppermute | solution.py:218
  33.2 1.1 %collective-permute-done.8 = f32[4,96,128]{2,1,0:T(8,128)S(1)} collective-permute-done((f32[4,96,128]{2,1,0:T(8,128)S(1)}, f32[4,96,128]{2,1,0:T(8,128)S(1)}, u32[]{:S(2)}, u32[]{:S(2)}) %collective-permute-start.8) | collective-permute-done | bytes 196640 | tf_op jit(solution)/shard_map/ppermute | solution.py:218
  34.3 2.6 %collective-permute-start.10 = (f32[96,128]{1,0:T(8,128)S(1)}, f32[96,128]{1,0:T(8,128)S(1)}, u32[]{:S(2)}, u32[]{:S(2)}) collective-permute-start(f32[96,128]{1,0:T(8,128)S(1)} %get-tuple-element.16), channel_id=1, source_target_pairs={{0,5},{1,4},{4,1},{5,0},{2,7},{3,6},{6,3},{7,2},{8,13},{9,12},{12,... | collective-permute-start | bytes 147464 | tf_op jit(solution)/shard_map/ppermute | solution.py:32
  36.9 0.5 %collective-permute-start.11 = (f32[96,128]{1,0:T(8,128)S(1)}, f32[96,128]{1,0:T(8,128)S(1)}, u32[]{:S(2)}, u32[]{:S(2)}) collective-permute-start(f32[96,128]{1,0:T(8,128)S(1)} %get-tuple-element.15), channel_id=1, source_target_pairs={{0,1},{1,0},{4,5},{5,4},{2,3},{3,2},{6,7},{7,6},{8,9},{9,8},{12,13... | collective-permute-start | bytes 147464 | tf_op jit(solution)/shard_map/ppermute | solution.py:32
  37.4 0.3 collective-permute-start.9
  37.6 0.9 %collective-permute-done.10.two_ref = f32[96,128]{1,0:T(8,128)S(1)} collective-permute-done((f32[96,128]{1,0:T(8,128)S(1)}, f32[96,128]{1,0:T(8,128)S(1)}, u32[]{:S(2)}, u32[]{:S(2)}) %collective-permute-start.10) | collective-permute-done | bytes 49184 | tf_op jit(solution)/shard_map/ppermute | solution.py:32
  38.5 2.8 %collective-permute-done.11.three_ref = f32[96,128]{1,0:T(8,128)S(1)} collective-permute-done((f32[96,128]{1,0:T(8,128)S(1)}, f32[96,128]{1,0:T(8,128)S(1)}, u32[]{:S(2)}, u32[]{:S(2)}) %collective-permute-start.11) | collective-permute-done | bytes 49184 | tf_op jit(solution)/shard_map/ppermute | solution.py:32
  41.3 0.0 collective-permute-done.9.one_ref
  41.3 1.0 %finish.1 = f32[6,2,48,96]{3,2,1,0:T(8,128)} custom-call(f32[1,96,128]{2,1,0:T(8,128)S(1)} %get-tuple-element.18.own_ref, f32[96,128]{1,0:T(8,128)S(1)} %collective-permute-done.9.one_ref, f32[96,128]{1,0:T(8,128)S(1)} %collective-permute-done.10.two_ref, f32[96,128]{1,0:T(8,128)S(1)} %collective-permute-done.11.three_ref), custom_call_target="tpu_custom_call" | custom-call | tf_op jit(solution)/shard_map/finish/pallas_call | solution.py:178
  (5 shorter events, 0.1 us)
Async XLA Ops:
  0.0 1.1 %copy-start = (bf16[24,16384]{1,0:T(8,128)(2,1)S(1)}, bf16[24,16384]{1,0:T(8,128)(2,1)}, u32[]{:S(2)}) copy-start(bf16[24,16384]{1,0:T(8,128)(2,1)} %param.1) | copy-start | bytes 2359300
  1.2 11.2 %collective-permute-start.4 = (bf16[24,4096]{1,0:T(8,128)(2,1)S(1)}, bf16[24,4096]{1,0:T(8,128)(2,1)S(1)}, u32[]{:S(2)}, u32[]{:S(2)}) collective-permute-start(bf16[24,4096]{1,0:T(8,128)(2,1)S(1)} %constant_dynamic-slice_fusion.2.refs_0_), channel_id=1, source_target_pairs={{0,8},{8,0},{16,24},{24,16},{32,40},{40,32},{48,56},{56,48},{64,72... | collective-permute-start | bytes 589832 | tf_op jit(solution)/shard_map/ppermute | solution.py:28
  3.7 12.2 %collective-permute-start.5 = (bf16[24,4096]{1,0:T(8,128)(2,1)S(1)}, bf16[24,4096]{1,0:T(8,128)(2,1)S(1)}, u32[]{:S(2)}, u32[]{:S(2)}) collective-permute-start(bf16[24,4096]{1,0:T(8,128)(2,1)S(1)} %constant_dynamic-slice_fusion.2.refs_0_), channel_id=1, source_target_pairs={{0,248},{8,16},{16,8},{24,32},{32,24},{40,48},{48,40},{56,64},{64,... | collective-permute-start | bytes 589832 | tf_op jit(solution)/shard_map/ppermute | solution.py:28
  10.8 5.2 %collective-permute-start = (bf16[24,4096]{1,0:T(8,128)(2,1)S(1)}, bf16[24,4096]{1,0:T(8,128)(2,1)S(1)}, u32[]{:S(2)}, u32[]{:S(2)}) collective-permute-start(bf16[24,4096]{1,0:T(8,128)(2,1)S(1)} %constant_dynamic-slice_fusion.1.refs_0_), channel_id=1, source_target_pairs={{0,8},{8,0},{16,24},{24,16},{32,40},{40,32},{48,56},{56,48},{64,72... | collective-permute-start | bytes 589832 | tf_op jit(solution)/shard_map/ppermute | solution.py:28
  10.9 9.1 %collective-permute-start.1 = (bf16[24,4096]{1,0:T(8,128)(2,1)S(1)}, bf16[24,4096]{1,0:T(8,128)(2,1)S(1)}, u32[]{:S(2)}, u32[]{:S(2)}) collective-permute-start(bf16[24,4096]{1,0:T(8,128)(2,1)S(1)} %constant_dynamic-slice_fusion.1.refs_0_), channel_id=1, source_target_pairs={{0,248},{8,16},{16,8},{24,32},{32,24},{40,48},{48,40},{56,64},{64,... | collective-permute-start | bytes 589832 | tf_op jit(solution)/shard_map/ppermute | solution.py:28
  12.4 11.3 %collective-permute-start.6 = (bf16[24,4096]{1,0:T(8,128)(2,1)S(1)}, bf16[24,4096]{1,0:T(8,128)(2,1)S(1)}, u32[]{:S(2)}, u32[]{:S(2)}) collective-permute-start(bf16[24,4096]{1,0:T(8,128)(2,1)S(1)} %collective-permute-done.4.refs_1_), channel_id=1, source_target_pairs={{0,248},{8,16},{16,8},{24,32},{32,24},{40,48},{48,40},{56,64},{64,... | collective-permute-start | bytes 589832 | tf_op jit(solution)/shard_map/ppermute | solution.py:28
  15.9 7.9 %collective-permute-start.7 = (bf16[24,4096]{1,0:T(8,128)(2,1)S(1)}, bf16[24,4096]{1,0:T(8,128)(2,1)S(1)}, u32[]{:S(2)}, u32[]{:S(2)}) collective-permute-start(bf16[24,4096]{1,0:T(8,128)(2,1)S(1)} %collective-permute-done.5.refs_2_), channel_id=1, source_target_pairs={{0,8},{8,0},{16,24},{24,16},{32,40},{40,32},{48,56},{56,48},{64,72... | collective-permute-start | bytes 589832 | tf_op jit(solution)/shard_map/ppermute | solution.py:28
  16.1 11.8 %collective-permute-start.2 = (bf16[24,4096]{1,0:T(8,128)(2,1)S(1)}, bf16[24,4096]{1,0:T(8,128)(2,1)S(1)}, u32[]{:S(2)}, u32[]{:S(2)}) collective-permute-start(bf16[24,4096]{1,0:T(8,128)(2,1)S(1)} %collective-permute-done.refs_1_), channel_id=1, source_target_pairs={{0,248},{8,16},{16,8},{24,32},{32,24},{40,48},{48,40},{56,64},{64,... | collective-permute-start | bytes 589832 | tf_op jit(solution)/shard_map/ppermute | solution.py:28
  20.1 7.9 %collective-permute-start.3 = (bf16[24,4096]{1,0:T(8,128)(2,1)S(1)}, bf16[24,4096]{1,0:T(8,128)(2,1)S(1)}, u32[]{:S(2)}, u32[]{:S(2)}) collective-permute-start(bf16[24,4096]{1,0:T(8,128)(2,1)S(1)} %collective-permute-done.1.refs_2_), channel_id=1, source_target_pairs={{0,8},{8,0},{16,24},{24,16},{32,40},{40,32},{48,56},{56,48},{64,72... | collective-permute-start | bytes 589832 | tf_op jit(solution)/shard_map/ppermute | solution.py:28
  30.9 3.4 %collective-permute-start.8 = (f32[4,96,128]{2,1,0:T(8,128)S(1)}, f32[4,96,128]{2,1,0:T(8,128)S(1)}, u32[]{:S(2)}, u32[]{:S(2)}) collective-permute-start(f32[4,96,128]{2,1,0:T(8,128)S(1)} %dynamic-slice_bitcast_fusion), channel_id=1, source_target_pairs={{0,2},{2,0},{1,3},{3,1},{4,6},{6,4},{5,7},{7,5},{8,10},{10,8},{9,1... | collective-permute-start | bytes 589832 | tf_op jit(solution)/shard_map/ppermute | solution.py:218
  34.3 4.2 %collective-permute-start.10 = (f32[96,128]{1,0:T(8,128)S(1)}, f32[96,128]{1,0:T(8,128)S(1)}, u32[]{:S(2)}, u32[]{:S(2)}) collective-permute-start(f32[96,128]{1,0:T(8,128)S(1)} %get-tuple-element.16), channel_id=1, source_target_pairs={{0,5},{1,4},{4,1},{5,0},{2,7},{3,6},{6,3},{7,2},{8,13},{9,12},{12,... | collective-permute-start | bytes 147464 | tf_op jit(solution)/shard_map/ppermute | solution.py:32
  36.9 4.4 %collective-permute-start.11 = (f32[96,128]{1,0:T(8,128)S(1)}, f32[96,128]{1,0:T(8,128)S(1)}, u32[]{:S(2)}, u32[]{:S(2)}) collective-permute-start(f32[96,128]{1,0:T(8,128)S(1)} %get-tuple-element.15), channel_id=1, source_target_pairs={{0,1},{1,0},{4,5},{5,4},{2,3},{3,2},{6,7},{7,6},{8,9},{9,8},{12,13... | collective-permute-start | bytes 147464 | tf_op jit(solution)/shard_map/ppermute | solution.py:32
  37.4 3.9 %collective-permute-start.9 = (f32[96,128]{1,0:T(8,128)S(1)}, f32[96,128]{1,0:T(8,128)S(1)}, u32[]{:S(2)}, u32[]{:S(2)}) collective-permute-start(f32[96,128]{1,0:T(8,128)S(1)} %get-tuple-element.17), channel_id=1, source_target_pairs={{0,4},{1,5},{4,0},{5,1},{2,6},{3,7},{6,2},{7,3},{8,12},{9,13},{12,... | collective-permute-start | bytes 147464 | tf_op jit(solution)/shard_map/ppermute | solution.py:32

commit v5 on v4

--- a/solution.py
+++ b/solution.py
@@ -67,26 +67,29 @@
             held_ref[...] = before[1][...] + second
 
 
-def row_of(i):
-    return i * 48 if i < STREAMED else CUT + (i - STREAMED) * 48
-
-
-def pack(acc_ref, out_ref):
+def rows(acc_ref, turned, at, count):
+    if at < CUT:
+        return acc_ref[at : at + count, :]
+    return turned[at - CUT : at - CUT + count]
+
+
+def pack(acc_ref, turned, out_ref):
     for core in range(2):
         for chip in range(4):
             xlo, rep = divmod(chip, 2)
             q = xlo * 2 + core
             for ii in range(3):
                 for half in range(2):
-                    row = row_of(SHARE * q + 3 * half + ii) + VB * rep
+                    i = SHARE * q + 3 * half + ii
+                    row = i * 48 + VB * rep + (48 if i >= STREAMED else 0)
                     out_ref[core, chip, ii * VB : (ii + 1) * VB, half * COLS : (half + 1) * COLS] = (
-                        acc_ref[row : row + VB, :]
+                        rows(acc_ref, turned, row, VB)
                     )
             out_ref[core, chip, 72:96, :COLS] = acc_ref[STREAMED * 48 + VB * rep : STREAMED * 48 + VB * (rep + 1), :]
             out_ref[core, chip, 72:80, COLS:] = jnp.concatenate(
                 [
-                    acc_ref[OWN + VB : OWN + VB + 1, :],
-                    acc_ref[OWN + SHARE * q : OWN + SHARE * (q + 1), :],
+                    rows(acc_ref, turned, OWN + VB, 1),
+                    rows(acc_ref, turned, OWN + SHARE * q, SHARE),
                     jnp.zeros((1, COLS), jnp.float32),
                 ],
                 axis=0,
@@ -114,10 +117,9 @@
             acc_ref, held_ref = refs
         accumulate(found, span, acc_ref, held_ref, before_refs)
         if last:
-            acc_ref[CUT:, :] = held_ref[...].T
-            pack(acc_ref, out_ref)
-
-    sums = [(CUT if not last else ROWS, COLS), (COLS, HELD)]
+            pack(acc_ref, held_ref[...].T, out_ref)
+
+    sums = [(CUT, COLS), (COLS, HELD)]
     packed = jax.ShapeDtypeStruct((2, 4, PACKED, 128), jnp.float32)
     width = span[1] - span[0]
     return pl.pallas_call(
@@ -143,9 +145,16 @@
     inside = same_half & (target < 96)
     entry = jnp.where(inside & (target // 2 == lane), jnp.where(even, -1.0, 1.0), 0.0)
     entry = entry + jnp.where(inside & even & (lane == 48), 2.0, 0.0)
-    spread = jnp.dot(
-        summed, entry, precision=lax.Precision.HIGHEST, preferred_element_type=jnp.float32
+    high = summed.astype(jnp.bfloat16)
+    rest = summed - high.astype(jnp.float32)
+    middle = rest.astype(jnp.bfloat16)
+    low = (rest - middle.astype(jnp.float32)).astype(jnp.bfloat16)
+    products = jnp.dot(
+        jnp.concatenate([high, middle, low], axis=0),
+        entry.astype(jnp.bfloat16),
+        preferred_element_type=jnp.float32,
     )
+    spread = products[:PACKED] + (products[PACKED : 2 * PACKED] + products[2 * PACKED :])
     third_row = spread[72:96, :96]
     singles = spread[72:80, 128:224]
     ones_row = singles[0:1]

time: 42.4 us -> 42.3 us (level)
  no operation moved by 1% of the time
where the time goes in v5:
time: 42.3 us; the launch traced here: 42.2 us
  starting transfers between devices  24.3 us (57%)
  waiting for transfers between devices  10.3 us (24%)
  Pallas kernels  6.28 us (15%)
  local copies, waits for them, and re-layouts  1.21 us (3%)
    ppermute x8, starting transfers between devices, swapped(): return lax.ppermute(value, 'vec', pairs)  18.7 us
    ppermute x8, waiting for transfers between devices, swapped(): return lax.ppermute(value, 'vec', pairs)  5.57 us
    pallas_call x2, Pallas kernels, tables_of(): pl.pallas_call(kernel, out_shape=packed if last else [jax.ShapeDtypeStruc...  5.34 us
    ppermute x3, waiting for transfers between devices, to_chip(): lax.ppermute(value, ('xlo', 'rep'), [(i, i ^ flip) for i in range(4)])  3.67 us
    ppermute x3, starting transfers between devices, to_chip(): lax.ppermute(value, ('xlo', 'rep'), [(i, i ^ flip) for i in range(4)])  3.34 us
    ppermute x1, starting transfers between devices, body(): kept = kept + lax.ppermute(sent, 'core', SWAP)  2.31 us
    unnamed x2, local copies, waits for them, and re-layouts  1.13 us
    ppermute x1, waiting for transfers between devices, body(): kept = kept + lax.ppermute(sent, 'core', SWAP)  1.07 us
  transfers between devices with their start and end apart: 12, of which 6 were waited for; matrix products, arithmetic and copies ran while one was open for 0% of the time, Pallas kernels for 6%

profile of v5, /device:TPU:1, one launch (start us, length us, event | category | flops | bytes accessed | tf_op | source)
XLA Modules:
  0.0 42.2 jit_solution(1188887201854907125)
XLA Ops:
  0.0 0.0 copy-start
  0.0 1.1 %copy-done = bf16[24,16384]{1,0:T(8,128)(2,1)S(1)} copy-done((bf16[24,16384]{1,0:T(8,128)(2,1)S(1)}, bf16[24,16384]{1,0:T(8,128)(2,1)}, u32[]{:S(2)}) %copy-start) | copy-done | bytes 786456
  1.2 2.6 %collective-permute-start.4 = (bf16[24,4096]{1,0:T(8,128)(2,1)S(1)}, bf16[24,4096]{1,0:T(8,128)(2,1)S(1)}, u32[]{:S(2)}, u32[]{:S(2)}) collective-permute-start(bf16[24,4096]{1,0:T(8,128)(2,1)S(1)} %constant_dynamic-slice_fusion.2.refs_0_), channel_id=1, source_target_pairs={{0,8},{8,0},{16,24},{24,16},{32,40},{40,32},{48,56},{56,48},{64,72... | collective-permute-start | bytes 589832 | tf_op jit(solution)/shard_map/ppermute | solution.py:28
  3.7 7.1 %collective-permute-start.5 = (bf16[24,4096]{1,0:T(8,128)(2,1)S(1)}, bf16[24,4096]{1,0:T(8,128)(2,1)S(1)}, u32[]{:S(2)}, u32[]{:S(2)}) collective-permute-start(bf16[24,4096]{1,0:T(8,128)(2,1)S(1)} %constant_dynamic-slice_fusion.2.refs_0_), channel_id=1, source_target_pairs={{0,248},{8,16},{16,8},{24,32},{32,24},{40,48},{48,40},{56,64},{64,... | collective-permute-start | bytes 589832 | tf_op jit(solution)/shard_map/ppermute | solution.py:28
  10.8 0.1 collective-permute-start
  10.9 1.4 %collective-permute-start.1 = (bf16[24,4096]{1,0:T(8,128)(2,1)S(1)}, bf16[24,4096]{1,0:T(8,128)(2,1)S(1)}, u32[]{:S(2)}, u32[]{:S(2)}) collective-permute-start(bf16[24,4096]{1,0:T(8,128)(2,1)S(1)} %constant_dynamic-slice_fusion.1.refs_0_), channel_id=1, source_target_pairs={{0,248},{8,16},{16,8},{24,32},{32,24},{40,48},{48,40},{56,64},{64,... | collective-permute-start | bytes 589832 | tf_op jit(solution)/shard_map/ppermute | solution.py:28
  12.4 0.0 collective-permute-done.4.refs_1_
  12.4 3.5 %collective-permute-start.6 = (bf16[24,4096]{1,0:T(8,128)(2,1)S(1)}, bf16[24,4096]{1,0:T(8,128)(2,1)S(1)}, u32[]{:S(2)}, u32[]{:S(2)}) collective-permute-start(bf16[24,4096]{1,0:T(8,128)(2,1)S(1)} %collective-permute-done.4.refs_1_), channel_id=1, source_target_pairs={{0,248},{8,16},{16,8},{24,32},{32,24},{40,48},{48,40},{56,64},{64,... | collective-permute-start | bytes 589832 | tf_op jit(solution)/shard_map/ppermute | solution.py:28
  15.9 0.0 collective-permute-done.5.refs_2_
  15.9 0.0 collective-permute-start.7
  15.9 0.2 collective-permute-done.refs_1_
  16.1 4.0 %collective-permute-start.2 = (bf16[24,4096]{1,0:T(8,128)(2,1)S(1)}, bf16[24,4096]{1,0:T(8,128)(2,1)S(1)}, u32[]{:S(2)}, u32[]{:S(2)}) collective-permute-start(bf16[24,4096]{1,0:T(8,128)(2,1)S(1)} %collective-permute-done.refs_1_), channel_id=1, source_target_pairs={{0,248},{8,16},{16,8},{24,32},{32,24},{40,48},{48,40},{56,64},{64,... | collective-permute-start | bytes 589832 | tf_op jit(solution)/shard_map/ppermute | solution.py:28
  20.1 0.0 collective-permute-done.1.refs_2_
  20.1 0.0 collective-permute-start.3
  20.1 3.6 %collective-permute-done.6.refs_3_ = bf16[24,4096]{1,0:T(8,128)(2,1)S(1)} collective-permute-done((bf16[24,4096]{1,0:T(8,128)(2,1)S(1)}, bf16[24,4096]{1,0:T(8,128)(2,1)S(1)}, u32[]{:S(2)}, u32[]{:S(2)}) %collective-permute-start.6) | collective-permute-done | bytes 196640 | tf_op jit(solution)/shard_map/ppermute | solution.py:28
  23.7 0.0 collective-permute-done.7.refs_4_
  23.7 2.5 %tables.2 = (f32[480,64]{1,0:T(8,128)S(1)}, f32[64,752]{1,0:T(8,128)S(1)}) custom-call(bf16[24,4096]{1,0:T(8,128)(2,1)S(1)} %constant_dynamic-slice_fusion.2.refs_0_, bf16[24,4096]{1,0:T(8,128)(2,1)S(1)} %collective-permute-done.4.refs_1_, bf16[24,4096]{1,0:T(8,128)(2,1)S(1)} %collective-permute-done.5.refs_2_, ...), custom_call_target="tpu_custom_call" | custom-call | flops 2583691264 | bytes 983040 | tf_op jit(solution)/shard_map/tables/pallas_call | solution.py:125
  26.2 1.7 %collective-permute-done.2.refs_3_ = bf16[24,4096]{1,0:T(8,128)(2,1)S(1)} collective-permute-done((bf16[24,4096]{1,0:T(8,128)(2,1)S(1)}, bf16[24,4096]{1,0:T(8,128)(2,1)S(1)}, u32[]{:S(2)}, u32[]{:S(2)}) %collective-permute-start.2) | collective-permute-done | bytes 196640 | tf_op jit(solution)/shard_map/ppermute | solution.py:28
  27.9 0.0 collective-permute-done.3.refs_4_
  27.9 2.9 %tables.3 = f32[2,4,96,128]{3,2,1,0:T(8,128)S(1)} custom-call(bf16[24,4096]{1,0:T(8,128)(2,1)S(1)} %constant_dynamic-slice_fusion.1.refs_0_, bf16[24,4096]{1,0:T(8,128)(2,1)S(1)} %collective-permute-done.refs_1_, bf16[24,4096]{1,0:T(8,128)(2,1)S(1)} %collective-permute-done.1.refs_2_, bf16[24,4096]{1,0:T(8,128)(2,1)S(1)} %collective-permute-done.2.refs_3_, ...), custom_call_target="tpu_custom_call" | custom-call | flops 2583691264 | bytes 983040 | tf_op jit(solution)/shard_map/tables/pallas_call | solution.py:125
  30.8 2.3 %collective-permute-start.8 = (f32[4,96,128]{2,1,0:T(8,128)S(1)}, f32[4,96,128]{2,1,0:T(8,128)S(1)}, u32[]{:S(2)}, u32[]{:S(2)}) collective-permute-start(f32[4,96,128]{2,1,0:T(8,128)S(1)} %dynamic-slice_bitcast_fusion), channel_id=1, source_target_pairs={{0,2},{2,0},{1,3},{3,1},{4,6},{6,4},{5,7},{7,5},{8,10},{10,8},{9,1... | collective-permute-start | bytes 589832 | tf_op jit(solution)/shard_map/ppermute | solution.py:227
  33.1 1.1 %collective-permute-done.8 = f32[4,96,128]{2,1,0:T(8,128)S(1)} collective-permute-done((f32[4,96,128]{2,1,0:T(8,128)S(1)}, f32[4,96,128]{2,1,0:T(8,128)S(1)}, u32[]{:S(2)}, u32[]{:S(2)}) %collective-permute-start.8) | collective-permute-done | bytes 196640 | tf_op jit(solution)/shard_map/ppermute | solution.py:227
  34.3 2.6 %collective-permute-start.10 = (f32[96,128]{1,0:T(8,128)S(1)}, f32[96,128]{1,0:T(8,128)S(1)}, u32[]{:S(2)}, u32[]{:S(2)}) collective-permute-start(f32[96,128]{1,0:T(8,128)S(1)} %get-tuple-element.16), channel_id=1, source_target_pairs={{0,5},{1,4},{4,1},{5,0},{2,7},{3,6},{6,3},{7,2},{8,13},{9,12},{12,... | collective-permute-start | bytes 147464 | tf_op jit(solution)/shard_map/ppermute | solution.py:32
  36.8 0.5 %collective-permute-start.11 = (f32[96,128]{1,0:T(8,128)S(1)}, f32[96,128]{1,0:T(8,128)S(1)}, u32[]{:S(2)}, u32[]{:S(2)}) collective-permute-start(f32[96,128]{1,0:T(8,128)S(1)} %get-tuple-element.15), channel_id=1, source_target_pairs={{0,1},{1,0},{4,5},{5,4},{2,3},{3,2},{6,7},{7,6},{8,9},{9,8},{12,13... | collective-permute-start | bytes 147464 | tf_op jit(solution)/shard_map/ppermute | solution.py:32
  37.4 0.3 collective-permute-start.9
  37.6 0.9 %collective-permute-done.10.two_ref = f32[96,128]{1,0:T(8,128)S(1)} collective-permute-done((f32[96,128]{1,0:T(8,128)S(1)}, f32[96,128]{1,0:T(8,128)S(1)}, u32[]{:S(2)}, u32[]{:S(2)}) %collective-permute-start.10) | collective-permute-done | bytes 49184 | tf_op jit(solution)/shard_map/ppermute | solution.py:32
  38.5 2.8 %collective-permute-done.11.three_ref = f32[96,128]{1,0:T(8,128)S(1)} collective-permute-done((f32[96,128]{1,0:T(8,128)S(1)}, f32[96,128]{1,0:T(8,128)S(1)}, u32[]{:S(2)}, u32[]{:S(2)}) %collective-permute-start.11) | collective-permute-done | bytes 49184 | tf_op jit(solution)/shard_map/ppermute | solution.py:32
  41.3 0.0 collective-permute-done.9.one_ref
  41.3 0.9 %finish.1 = f32[6,2,48,96]{3,2,1,0:T(8,128)} custom-call(f32[1,96,128]{2,1,0:T(8,128)S(1)} %get-tuple-element.18.own_ref, f32[96,128]{1,0:T(8,128)S(1)} %collective-permute-done.9.one_ref, f32[96,128]{1,0:T(8,128)S(1)} %collective-permute-done.10.two_ref, f32[96,128]{1,0:T(8,128)S(1)} %collective-permute-done.11.three_ref), custom_call_target="tpu_custom_call" | custom-call | tf_op jit(solution)/shard_map/finish/pallas_call | solution.py:187
  (5 shorter events, 0.1 us)
Async XLA Ops:
  0.0 1.1 %copy-start = (bf16[24,16384]{1,0:T(8,128)(2,1)S(1)}, bf16[24,16384]{1,0:T(8,128)(2,1)}, u32[]{:S(2)}) copy-start(bf16[24,16384]{1,0:T(8,128)(2,1)} %param.1) | copy-start | bytes 2359300
  1.2 11.2 %collective-permute-start.4 = (bf16[24,4096]{1,0:T(8,128)(2,1)S(1)}, bf16[24,4096]{1,0:T(8,128)(2,1)S(1)}, u32[]{:S(2)}, u32[]{:S(2)}) collective-permute-start(bf16[24,4096]{1,0:T(8,128)(2,1)S(1)} %constant_dynamic-slice_fusion.2.refs_0_), channel_id=1, source_target_pairs={{0,8},{8,0},{16,24},{24,16},{32,40},{40,32},{48,56},{56,48},{64,72... | collective-permute-start | bytes 589832 | tf_op jit(solution)/shard_map/ppermute | solution.py:28
  3.7 12.2 %collective-permute-start.5 = (bf16[24,4096]{1,0:T(8,128)(2,1)S(1)}, bf16[24,4096]{1,0:T(8,128)(2,1)S(1)}, u32[]{:S(2)}, u32[]{:S(2)}) collective-permute-start(bf16[24,4096]{1,0:T(8,128)(2,1)S(1)} %constant_dynamic-slice_fusion.2.refs_0_), channel_id=1, source_target_pairs={{0,248},{8,16},{16,8},{24,32},{32,24},{40,48},{48,40},{56,64},{64,... | collective-permute-start | bytes 589832 | tf_op jit(solution)/shard_map/ppermute | solution.py:28
  10.8 5.2 %collective-permute-start = (bf16[24,4096]{1,0:T(8,128)(2,1)S(1)}, bf16[24,4096]{1,0:T(8,128)(2,1)S(1)}, u32[]{:S(2)}, u32[]{:S(2)}) collective-permute-start(bf16[24,4096]{1,0:T(8,128)(2,1)S(1)} %constant_dynamic-slice_fusion.1.refs_0_), channel_id=1, source_target_pairs={{0,8},{8,0},{16,24},{24,16},{32,40},{40,32},{48,56},{56,48},{64,72... | collective-permute-start | bytes 589832 | tf_op jit(solution)/shard_map/ppermute | solution.py:28
  10.9 9.1 %collective-permute-start.1 = (bf16[24,4096]{1,0:T(8,128)(2,1)S(1)}, bf16[24,4096]{1,0:T(8,128)(2,1)S(1)}, u32[]{:S(2)}, u32[]{:S(2)}) collective-permute-start(bf16[24,4096]{1,0:T(8,128)(2,1)S(1)} %constant_dynamic-slice_fusion.1.refs_0_), channel_id=1, source_target_pairs={{0,248},{8,16},{16,8},{24,32},{32,24},{40,48},{48,40},{56,64},{64,... | collective-permute-start | bytes 589832 | tf_op jit(solution)/shard_map/ppermute | solution.py:28
  12.4 11.3 %collective-permute-start.6 = (bf16[24,4096]{1,0:T(8,128)(2,1)S(1)}, bf16[24,4096]{1,0:T(8,128)(2,1)S(1)}, u32[]{:S(2)}, u32[]{:S(2)}) collective-permute-start(bf16[24,4096]{1,0:T(8,128)(2,1)S(1)} %collective-permute-done.4.refs_1_), channel_id=1, source_target_pairs={{0,248},{8,16},{16,8},{24,32},{32,24},{40,48},{48,40},{56,64},{64,... | collective-permute-start | bytes 589832 | tf_op jit(solution)/shard_map/ppermute | solution.py:28
  15.9 7.9 %collective-permute-start.7 = (bf16[24,4096]{1,0:T(8,128)(2,1)S(1)}, bf16[24,4096]{1,0:T(8,128)(2,1)S(1)}, u32[]{:S(2)}, u32[]{:S(2)}) collective-permute-start(bf16[24,4096]{1,0:T(8,128)(2,1)S(1)} %collective-permute-done.5.refs_2_), channel_id=1, source_target_pairs={{0,8},{8,0},{16,24},{24,16},{32,40},{40,32},{48,56},{56,48},{64,72... | collective-permute-start | bytes 589832 | tf_op jit(solution)/shard_map/ppermute | solution.py:28
  16.1 11.8 %collective-permute-start.2 = (bf16[24,4096]{1,0:T(8,128)(2,1)S(1)}, bf16[24,4096]{1,0:T(8,128)(2,1)S(1)}, u32[]{:S(2)}, u32[]{:S(2)}) collective-permute-start(bf16[24,4096]{1,0:T(8,128)(2,1)S(1)} %collective-permute-done.refs_1_), channel_id=1, source_target_pairs={{0,248},{8,16},{16,8},{24,32},{32,24},{40,48},{48,40},{56,64},{64,... | collective-permute-start | bytes 589832 | tf_op jit(solution)/shard_map/ppermute | solution.py:28
  20.1 7.9 %collective-permute-start.3 = (bf16[24,4096]{1,0:T(8,128)(2,1)S(1)}, bf16[24,4096]{1,0:T(8,128)(2,1)S(1)}, u32[]{:S(2)}, u32[]{:S(2)}) collective-permute-start(bf16[24,4096]{1,0:T(8,128)(2,1)S(1)} %collective-permute-done.1.refs_2_), channel_id=1, source_target_pairs={{0,8},{8,0},{16,24},{24,16},{32,40},{40,32},{48,56},{56,48},{64,72... | collective-permute-start | bytes 589832 | tf_op jit(solution)/shard_map/ppermute | solution.py:28
  30.8 3.4 %collective-permute-start.8 = (f32[4,96,128]{2,1,0:T(8,128)S(1)}, f32[4,96,128]{2,1,0:T(8,128)S(1)}, u32[]{:S(2)}, u32[]{:S(2)}) collective-permute-start(f32[4,96,128]{2,1,0:T(8,128)S(1)} %dynamic-slice_bitcast_fusion), channel_id=1, source_target_pairs={{0,2},{2,0},{1,3},{3,1},{4,6},{6,4},{5,7},{7,5},{8,10},{10,8},{9,1... | collective-permute-start | bytes 589832 | tf_op jit(solution)/shard_map/ppermute | solution.py:227
  34.3 4.2 %collective-permute-start.10 = (f32[96,128]{1,0:T(8,128)S(1)}, f32[96,128]{1,0:T(8,128)S(1)}, u32[]{:S(2)}, u32[]{:S(2)}) collective-permute-start(f32[96,128]{1,0:T(8,128)S(1)} %get-tuple-element.16), channel_id=1, source_target_pairs={{0,5},{1,4},{4,1},{5,0},{2,7},{3,6},{6,3},{7,2},{8,13},{9,12},{12,... | collective-permute-start | bytes 147464 | tf_op jit(solution)/shard_map/ppermute | solution.py:32
  36.8 4.4 %collective-permute-start.11 = (f32[96,128]{1,0:T(8,128)S(1)}, f32[96,128]{1,0:T(8,128)S(1)}, u32[]{:S(2)}, u32[]{:S(2)}) collective-permute-start(f32[96,128]{1,0:T(8,128)S(1)} %get-tuple-element.15), channel_id=1, source_target_pairs={{0,1},{1,0},{4,5},{5,4},{2,3},{3,2},{6,7},{7,6},{8,9},{9,8},{12,13... | collective-permute-start | bytes 147464 | tf_op jit(solution)/shard_map/ppermute | solution.py:32
  37.4 3.9 %collective-permute-start.9 = (f32[96,128]{1,0:T(8,128)S(1)}, f32[96,128]{1,0:T(8,128)S(1)}, u32[]{:S(2)}, u32[]{:S(2)}) collective-permute-start(f32[96,128]{1,0:T(8,128)S(1)} %get-tuple-element.17), channel_id=1, source_target_pairs={{0,4},{1,5},{4,0},{5,1},{2,6},{3,7},{6,2},{7,3},{8,12},{9,13},{12,... | collective-permute-start | bytes 147464 | tf_op jit(solution)/shard_map/ppermute | solution.py:32
